TPU v7x, 128 devices: a whole 4x4x4 slice. The times are simulated.
128 devices in a mesh: tm: 32 (over y, z, core), tp: 4 (over x).
Axes of the slice: x: 4, y: 4, z: 4, core: 2. Of those that a mesh axis runs over, the one named last changes fastest.
Arguments:
- latents: bfloat16 [64, 128, 5120], P('tm', None, 'tp'), may hold values from -30 to 30
- noise: bfloat16 [64, 128, 5120], P('tm', None, 'tp'), may hold values from -6 to 6
- mod_table: bfloat16 [256, 15360], replicated, may hold values from -0.375 to 0.375
- w_query: bfloat16 [5120, 2560], P('tm', 'tp'), may hold values from -4 to 4
- w_key: bfloat16 [5120, 2560], P('tm', 'tp'), may hold values from -4 to 4
- w_value: bfloat16 [5120, 2560], P('tm', 'tp'), may hold values from -0.078125 to 0.078125
- w_out: bfloat16 [2560, 5120], P('tp', 'tm'), may hold values from -0.125 to 0.125
- step_index: int32 [64], P('tm'), may hold values from 0 to 999
- slide_offset: int32 [], replicated, may hold values from 1 to 2
Outputs:
- window: bfloat16 [64, 128, 5120], P('tm', None, 'tp')
All inputs are finite; a program needn't handle non-finite values.
Results may differ from a plain program's by a relative error of at most 0.017.
Values may be sent and summed in bfloat16 or wider, within the bound.
A program may use at most 128 MiB of HBM per device.

v0:
```python
import math

import jax
import jax.numpy as jnp
from jax import lax
from jax.sharding import PartitionSpec as P

HEAD_SIZE = 128
ITERS = 2


def prefix_2(x, axis, combine, identity):
    size, here = (lax.axis_size(axis), lax.axis_index(axis))
    everything = lax.all_gather(x.astype(jnp.bfloat16), axis)
    start = jnp.broadcast_to(jnp.asarray(identity, x.dtype), x.shape)

    def step(k, before):
        reached = k < here
        new = combine(before, everything[k].astype(x.dtype))
        return jnp.where(reached, new, before)

    return lax.fori_loop(0, size, step, start)


def passed_along(block, axis, distance):
    devices = range(lax.axis_size(axis))
    route = [(i - distance, i) for i in devices if i - distance in devices]
    return lax.ppermute(block, axis, route)


def modulate(step_index, mod_table):
    half = mod_table.shape[0] // 2
    freqs = jnp.exp(-math.log(10000.0) * jnp.arange(half).astype(jnp.float32) / half)
    angles = step_index.astype(jnp.float32)[:, None] * freqs[None, :]
    feats = jnp.concatenate([jnp.cos(angles), jnp.sin(angles)], axis=1).astype(jnp.bfloat16)
    return jnp.dot(feats, mod_table, preferred_element_type=jnp.float32)


def attention_part(whole, shift, scale, full_query, full_key, full_value, full_out):
    steps, tokens, width = whole.shape
    local_width = full_query.shape[1]
    local_heads = local_width // HEAD_SIZE
    rows = whole.astype(jnp.float32)
    mean = jnp.mean(rows, axis=-1, keepdims=True)
    centred = rows - mean
    var = jnp.mean(centred * centred, axis=-1, keepdims=True)
    normed = centred * lax.rsqrt(var + 1e-06)
    inputs = (normed * (1.0 + scale[:, None, :]) + shift[:, None, :]).astype(jnp.bfloat16)
    inputs = inputs.reshape(steps * tokens, width)
    shape_four = (steps, tokens, local_heads, HEAD_SIZE)
    query_rows = (
        jnp.dot(inputs, full_query, preferred_element_type=jnp.float32)
        .astype(jnp.bfloat16)
        .reshape(shape_four)
    )
    key_rows = (
        jnp.dot(inputs, full_key, preferred_element_type=jnp.float32)
        .astype(jnp.bfloat16)
        .reshape(shape_four)
    )
    value_rows = (
        jnp.dot(inputs, full_value, preferred_element_type=jnp.float32)
        .astype(jnp.bfloat16)
        .reshape(shape_four)
    )
    score_matrix = jnp.einsum(
        "slhd,smhd->shlm", query_rows, key_rows, preferred_element_type=jnp.float32
    ) * (1.0 / math.sqrt(HEAD_SIZE))
    top = jnp.max(score_matrix, axis=-1, keepdims=True)
    expo = jnp.exp(score_matrix - top)
    attention_probabilities = (expo / jnp.sum(expo, axis=-1, keepdims=True)).astype(jnp.bfloat16)
    head_outputs = jnp.einsum(
        "shlm,smhd->slhd", attention_probabilities, value_rows, preferred_element_type=jnp.float32
    ).astype(jnp.bfloat16)
    head_outputs = head_outputs.reshape(steps * tokens, local_width)
    partial_value = jnp.dot(head_outputs, full_out, preferred_element_type=jnp.float32)
    return partial_value.reshape(steps, tokens, width)


def exclusive_local(terms):
    running = jnp.cumsum(terms, axis=0)
    return (jnp.concatenate([jnp.zeros_like(terms[:1]), running[:-1]], axis=0), running[-1])


def per_device(latents, noise, mod_table, w_query, w_key, w_value, w_out, step_index, slide_offset):
    parts = lax.axis_size("tm")
    rank = lax.axis_index("tm")
    tp_rank = lax.axis_index("tp")
    steps, tokens, quarter = latents.shape
    width = mod_table.shape[1] // 3
    full_query, full_key, full_value, full_out = (
        lax.all_gather(w_query, "tm", axis=0, tiled=True),
        lax.all_gather(w_key, "tm", axis=0, tiled=True),
        lax.all_gather(w_value, "tm", axis=0, tiled=True),
        lax.all_gather(w_out, "tm", axis=1, tiled=True),
    )
    modulation = modulate(step_index, mod_table)
    shift = modulation[:, :width]
    scale = modulation[:, width : 2 * width]
    gate = lax.dynamic_slice_in_dim(modulation[:, 2 * width :], tp_rank * quarter, quarter, 1)
    step_size = (step_index.astype(jnp.float32) + 1.0) / 2000.0
    noise_size = 0.2 * jnp.sqrt(step_size)
    noise_terms = noise_size[:, None, None] * noise.astype(jnp.float32)
    first = jnp.where(
        rank == 0, latents[0].astype(jnp.float32), jnp.zeros((tokens, quarter), jnp.float32)
    )
    current = latents
    terms = None
    device_term = None
    prefix = None
    for iteration in range(ITERS):
        whole = lax.all_gather(current, "tp", axis=2, tiled=True)
        partial_value = attention_part(
            whole, shift, scale, full_query, full_key, full_value, full_out
        )
        attn = lax.psum_scatter(
            partial_value.astype(jnp.bfloat16), "tp", scatter_dimension=2, tiled=True
        ).astype(jnp.float32)
        terms = step_size[:, None, None] * gate[:, None, :] * attn + noise_terms
        before, total = exclusive_local(terms)
        device_term = total + first
        prefix = prefix_2(
            device_term,
            "tm",
            lambda earlier, later: earlier + later,
            jnp.zeros((tokens, quarter), jnp.float32),
        )
        current = (prefix[None] + first[None] + before).astype(jnp.bfloat16)
    following = passed_along(current, "tm", -1)
    fill = jnp.broadcast_to(current[-1:], current.shape)
    following = jnp.where(rank == parts - 1, fill, following)
    joined = jnp.concatenate([current, following], axis=0)
    return lax.dynamic_slice_in_dim(joined, slide_offset, steps, 0)


def solution(mesh):
    placed = (
        P("tm", None, "tp"),
        P("tm", None, "tp"),
        P(),
        P("tm", "tp"),
        P("tm", "tp"),
        P("tm", "tp"),
        P("tp", "tm"),
        P("tm"),
        P(),
    )
    return jax.shard_map(
        per_device, mesh=mesh, in_specs=placed, out_specs=P("tm", None, "tp"), check_vma=False
    )
```

profile of v0, /device:TPU:1, one launch (start us, length us, event | category | flops | bytes accessed | tf_op | source)
XLA Modules:
  0.0 628.6 jit_solution(12798240022268133765)
XLA Ops:
  10.7 4.4 fusion.53
  15.1 32.3 %all-gather.9.cloned.1.call-done = bf16[2,128,5120]{2,1,0:T(8,128)(2,1)} async-done(((bf16[2,128,1280]{2,1,0:T(8,128)(2,1)}), bf16[2,128,5120]{2,1,0:T(8,128)(2,1)}) %all-gather.9.cloned.1.call-update) | async-done | bytes 2621456 | tf_op jit(solution)/shard_map/all_gather | solution.py:112
  47.4 2.3 convert_reduce_fusion.1
  49.8 2.6 fusion.20
  53.7 46.3 %all-gather.13.cloned.1.call-done = bf16[5120,640]{1,0:T(8,128)(2,1)} async-done(((bf16[160,640]{1,0:T(8,128)(2,1)}), bf16[5120,640]{1,0:T(8,128)(2,1)}) %all-gather.13.cloned.1.call-update) | async-done | bytes 6553616 | tf_op jit(solution)/shard_map/all_gather | solution.py:92
  100.0 5.8 convolution_convert_fusion.4
  105.8 1.3 reshape.102
  107.1 43.6 %all-gather.15.cloned.1.call-done = bf16[5120,640]{1,0:T(8,128)(2,1)} async-done(((bf16[160,640]{1,0:T(8,128)(2,1)}), bf16[5120,640]{1,0:T(8,128)(2,1)}) %all-gather.15.cloned.1.call-update) | async-done | bytes 6553616 | tf_op jit(solution)/shard_map/all_gather | solution.py:93
  150.7 5.8 convolution_convert_fusion.3
  156.5 2.1 reshape.103
  158.6 42.7 %all-gather.11.cloned.1.call-done = bf16[5120,640]{1,0:T(8,128)(2,1)} async-done(((bf16[160,640]{1,0:T(8,128)(2,1)}), bf16[5120,640]{1,0:T(8,128)(2,1)}) %all-gather.11.cloned.1.call-update) | async-done | bytes 6553616 | tf_op jit(solution)/shard_map/all_gather | solution.py:94
  201.3 5.8 convolution_convert_fusion.5
  207.1 1.3 reshape.101
  208.4 1.5 fusion.71
  209.9 1.4 convolution_multiply_fusion.1
  211.7 40.2 %all-gather.17.cloned.1.call-done = bf16[640,5120]{0,1:T(8,128)(2,1)} async-done(((bf16[640,160]{0,1:T(8,128)(2,1)}), bf16[640,5120]{0,1:T(8,128)(2,1)}) %all-gather.17.cloned.1.call-update) | async-done | bytes 6553616 | tf_op jit(solution)/shard_map/all_gather | solution.py:95
  251.9 6.7 %fusion.6 = bf16[2,128,5120]{2,1,0:T(8,128)(2,1)} fusion(bf16[2,128,640]{1,2,0:T(8,128)(2,1)S(1)} %bitcast.55, bf16[640,5120]{0,1:T(8,128)(2,1)} %all-gather.17.cloned.1.call-done), kind=kOutput, calls=%fused_computation.12 | convolution fusion | flops 1679032320 | bytes 9502720 | tf_op jit(solution)/shard_map/dot_general | solution.py:76
  258.8 32.3 %reduce-scatter.3.cloned.1.call-done = bf16[2,128,1280]{2,1,0:T(8,128)(2,1)} async-done(((bf16[2,128,5120]{2,1,0:T(8,128)(2,1)}), bf16[2,128,1280]{2,1,0:T(8,128)(2,1)}) %reduce-scatter.3.cloned.1.call-update) | async-done | bytes 655376 | tf_op jit(solution)/shard_map/reduce_scatter | solution.py:116
  291.0 1.4 fusion.30
  293.3 58.2 %all-gather.19.cloned.1.call-done = bf16[32,128,1280]{2,1,0:T(8,128)(2,1)} async-done(((bf16[1,128,1280]{2,1,0:T(8,128)(2,1)}), bf16[32,128,1280]{2,1,0:T(8,128)(2,1)}) %all-gather.19.cloned.1.call-update) | async-done | bytes 10485776 | tf_op jit(solution)/shard_map/all_gather | solution.py:14
  351.5 42.7 %while.28 = (s32[]{:T(128)}, f32[128,1280]{1,0:T(8,128)S(1)}, s32[]{:T(128)}, bf16[32,128,1280]{2,1,0:T(8,128)(2,1)}, s32[]{:T(128)}, /*index=5*/s32[]{:T(128)}) while((s32[]{:T(128)}, f32[128,1280]{1,0:T(8,128)S(1)}, s32[]{:T(128)}, bf16[32,128,1280]{2,1,0:T(8,128)(2,1)}, s32[]{:T(128)}, /*index=5*/s32[]{:T(128)}) %tuple.65), condition=%wide.region_7.8_spmd.clone, body=%wide.region_6.7_spmd.clone.sunk | while | flops 655364 | bytes 1638493 | solution.py:22
  352.8 1.3 add_select_fusion.4
  355.5 1.3 add_select_fusion.4
  356.8 1.3 add_select_fusion.4
  358.1 1.3 add_select_fusion.4
  362.1 1.3 add_select_fusion.4
  363.5 1.3 add_select_fusion.4
  364.8 1.3 add_select_fusion.4
  368.8 1.3 add_select_fusion.4
  370.2 1.3 add_select_fusion.4
  371.5 1.3 add_select_fusion.4
  375.5 1.3 add_select_fusion.4
  376.8 1.3 add_select_fusion.4
  378.2 1.3 add_select_fusion.4
  380.8 1.3 add_select_fusion.4
  382.2 1.3 add_select_fusion.4
  383.5 1.3 add_select_fusion.4
  387.5 1.3 add_select_fusion.4
  388.8 1.3 add_select_fusion.4
  390.2 1.3 add_select_fusion.4
  395.4 34.1 %all-gather.21.cloned.1.call-done = bf16[2,128,5120]{2,1,0:T(8,128)(2,1)} async-done(((bf16[2,128,1280]{2,1,0:T(8,128)(2,1)}), bf16[2,128,5120]{2,1,0:T(8,128)(2,1)}) %all-gather.21.cloned.1.call-update) | async-done | bytes 2621456 | tf_op jit(solution)/shard_map/all_gather | solution.py:112
  429.5 2.3 convert_reduce_fusion
  431.8 2.6 fusion.16
  435.7 5.8 convolution_convert_fusion.1
  441.5 2.1 reshape.105
  443.7 5.8 convolution_convert_fusion
  449.5 2.1 reshape.106
  451.6 2.4 convolution_multiply_fusion
  454.0 1.6 fusion.76
  455.6 5.8 convolution_convert_fusion.2
  461.4 1.3 reshape.104
  462.7 1.7 convolution_convert_fusion.6
  464.5 6.7 %fusion.9 = bf16[2,128,5120]{2,1,0:T(8,128)(2,1)} fusion(bf16[2,128,640]{1,2,0:T(8,128)(2,1)S(1)} %bitcast.56, bf16[640,5120]{0,1:T(8,128)(2,1)} %all-gather.17.cloned.1.call-done), kind=kOutput, calls=%fused_computation.13 | convolution fusion | flops 1679032320 | bytes 9502720 | tf_op jit(solution)/shard_map/dot_general | solution.py:76
  471.2 34.2 %reduce-scatter.5.cloned.1.call-done = bf16[2,128,1280]{2,1,0:T(8,128)(2,1)} async-done(((bf16[2,128,5120]{2,1,0:T(8,128)(2,1)}), bf16[2,128,1280]{2,1,0:T(8,128)(2,1)}) %reduce-scatter.5.cloned.1.call-update) | async-done | bytes 655376 | tf_op jit(solution)/shard_map/reduce_scatter | solution.py:116
  505.5 1.4 fusion.26
  507.7 58.2 %all-gather.23.cloned.1.call-done = bf16[32,128,1280]{2,1,0:T(8,128)(2,1)} async-done(((bf16[1,128,1280]{2,1,0:T(8,128)(2,1)}), bf16[32,128,1280]{2,1,0:T(8,128)(2,1)}) %all-gather.23.cloned.1.call-update) | async-done | bytes 10485776 | tf_op jit(solution)/shard_map/all_gather | solution.py:14
  565.9 42.7 %while.29 = (s32[]{:T(128)}, f32[128,1280]{1,0:T(8,128)S(1)}, s32[]{:T(128)}, bf16[32,128,1280]{2,1,0:T(8,128)(2,1)}, s32[]{:T(128)}, /*index=5*/s32[]{:T(128)}) while((s32[]{:T(128)}, f32[128,1280]{1,0:T(8,128)S(1)}, s32[]{:T(128)}, bf16[32,128,1280]{2,1,0:T(8,128)(2,1)}, s32[]{:T(128)}, /*index=5*/s32[]{:T(128)}) %tuple.68), condition=%wide.region_15.16_spmd.clone, body=%wide.region_14.15_spmd.clone.sunk | while | flops 655364 | bytes 1638493 | solution.py:22
  567.2 1.3 add_select_fusion.5
  568.6 1.3 add_select_fusion.5
  569.9 1.3 add_select_fusion.5
  573.9 1.3 add_select_fusion.5
  575.2 1.3 add_select_fusion.5
  608.7 2.2 collective-permute-start
  611.6 9.1 %collective-permute-done = bf16[2,128,1280]{2,1,0:T(8,128)(2,1)S(1)} collective-permute-done((bf16[2,128,1280]{2,1,0:T(8,128)(2,1)S(1)}, bf16[2,128,1280]{2,1,0:T(8,128)(2,1)S(1)}, u32[]{:S(2)}, u32[]{:S(2)}) %collective-permute-start) | collective-permute-done | bytes 655392 | tf_op jit(solution)/shard_map/ppermute | solution.py:28
  (96 shorter events, 64.1 us)
Async XLA Ops:
  6.5 40.9 %all-gather.9.cloned.1.call-start = ((), (), s32[]{:S(2)}) async-start(), calls=%async_computation.2 | async-start | bytes 3276800 | tf_op jit(solution)/shard_map/all_gather | solution.py:112
  7.3 92.7 %all-gather.13.cloned.1.call-start = ((), (), s32[]{:S(2)}) async-start(), calls=%async_computation.4 | async-start | bytes 6758400 | tf_op jit(solution)/shard_map/all_gather | solution.py:92
  8.0 142.7 %all-gather.15.cloned.1.call-start = ((), (), s32[]{:S(2)}) async-start(), calls=%async_computation.5 | async-start | bytes 6758400 | tf_op jit(solution)/shard_map/all_gather | solution.py:93
  8.7 192.6 %all-gather.11.cloned.1.call-start = ((), (), s32[]{:S(2)}) async-start(), calls=%async_computation.3 | async-start | bytes 6758400 | tf_op jit(solution)/shard_map/all_gather | solution.py:94
  9.3 242.6 %all-gather.17.cloned.1.call-start = ((), (), s32[]{:S(2)}) async-start(), calls=%async_computation.6 | async-start | bytes 6758400 | tf_op jit(solution)/shard_map/all_gather | solution.py:95
  9.9 281.1 %reduce-scatter.3.cloned.1.call-start = ((), (), s32[]{:S(2)}) async-start(), calls=%async_computation.7 | async-start | bytes 3276800 | tf_op jit(solution)/shard_map/reduce_scatter | solution.py:116
  47.4 4.9 copy-start
  251.9 6.8 %copy-start.5 = (s32[2]{0:T(128)S(1)}, s32[2]{0:T(128)}, u32[]{:S(2)}) copy-start(s32[2]{0:T(128)} %param.20) | copy-start | bytes 28
  251.9 39.1 %copy-start.3 = (bf16[2,128,1280]{2,1,0:T(8,128)(2,1)S(1)}, bf16[2,128,1280]{2,1,0:T(8,128)(2,1)}, u32[]{:S(2)}) copy-start(bf16[2,128,1280]{2,1,0:T(8,128)(2,1)} %param.14) | copy-start | bytes 1966084
  258.6 33.8 %copy-start.2 = (bf16[2,128,1280]{2,1,0:T(8,128)(2,1)S(1)}, bf16[2,128,1280]{2,1,0:T(8,128)(2,1)}, u32[]{:S(2)}) copy-start(bf16[2,128,1280]{2,1,0:T(8,128)(2,1)} %param.13) | copy-start | bytes 1966084
  258.6 92.9 %all-gather.19.cloned.1.call-start = ((), (), s32[]{:S(2)}) async-start(), calls=%async_computation.8 | async-start | bytes 10813440 | tf_op jit(solution)/shard_map/all_gather | solution.py:14
  293.3 136.2 %all-gather.21.cloned.1.call-start = ((), (), s32[]{:S(2)}) async-start(), calls=%async_computation.9 | async-start | bytes 3276800 | tf_op jit(solution)/shard_map/all_gather | solution.py:112
  395.2 110.3 %reduce-scatter.5.cloned.1.call-start = ((), (), s32[]{:S(2)}) async-start(), calls=%async_computation.10 | async-start | bytes 3276800 | tf_op jit(solution)/shard_map/reduce_scatter | solution.py:116
  429.5 4.9 copy-start.1
  464.5 41.0 %copy-start.4 = (bf16[2,128,1280]{2,1,0:T(8,128)(2,1)S(1)}, bf16[2,128,1280]{2,1,0:T(8,128)(2,1)}, u32[]{:S(2)}) copy-start(bf16[2,128,1280]{2,1,0:T(8,128)(2,1)} %param.14) | copy-start | bytes 1966084
  471.2 94.7 %all-gather.23.cloned.1.call-start = ((), (), s32[]{:S(2)}) async-start(), calls=%async_computation.11 | async-start | bytes 10813440 | tf_op jit(solution)/shard_map/all_gather | solution.py:14
  608.7 11.9 %collective-permute-start = (bf16[2,128,1280]{2,1,0:T(8,128)(2,1)S(1)}, bf16[2,128,1280]{2,1,0:T(8,128)(2,1)S(1)}, u32[]{:S(2)}, u32[]{:S(2)}) collective-permute-start(bf16[2,128,1280]{2,1,0:T(8,128)(2,1)S(1)} %add_convert_fusion), channel_id=1, source_target_pairs={{4,0},{8,4},{12,8},{16,12},{20,16},{24,20},{28,24},{32,28},{36,32}... | collective-permute-start | bytes 1966088 | tf_op jit(solution)/shard_map/ppermute | solution.py:28
Sparse Core Ops, SparseCore 0:
  9.0 38.3 all-gather.8
  49.7 50.2 all-gather.12
  102.2 48.4 all-gather.14
  152.8 48.4 all-gather.10
  203.4 48.4 all-gather.16
  258.7 32.2 reduce-scatter.2
  293.4 58.0 all-gather.18
  395.3 34.1 all-gather.20
  471.3 34.0 reduce-scatter.4
  507.8 58.0 all-gather.22
where the time goes:
time: 632 us; the launch traced here: 629 us
  waiting for transfers between devices  434 us (69%)
  other arithmetic  104 us (16%)
  matrix products  61.4 us (10%)
  between operations  14.4 us (2%)
  local copies, waits for them, and re-layouts  10.5 us (2%)
    all_gather x2, waiting for transfers between devices, prefix_2(): everything = lax.all_gather(x.astype(jnp.bfloat16), axis)  116 us
    select_n x64, other arithmetic, step(): return jnp.where(reached, new, before)  83.9 us
    reduce_scatter x2, waiting for transfers between devices, per_device(): lax.psum_scatter(partial_value.astype(jnp.bfloat16), 'tp', scatter_dimens...  66.5 us
    all_gather x2, waiting for transfers between devices, per_device(): whole = lax.all_gather(current, 'tp', axis=2, tiled=True)  66.4 us
    all_gather x1, waiting for transfers between devices, per_device(): lax.all_gather(w_query, 'tm', axis=0, tiled=True)  46.3 us
    all_gather x1, waiting for transfers between devices, per_device(): lax.all_gather(w_key, 'tm', axis=0, tiled=True)  43.6 us
    all_gather x1, waiting for transfers between devices, per_device(): lax.all_gather(w_value, 'tm', axis=0, tiled=True)  42.7 us
    all_gather x1, waiting for transfers between devices, per_device(): lax.all_gather(w_out, 'tm', axis=1, tiled=True)  40.2 us
  transfers between devices with their start and end apart: 11, of which 11 were waited for; matrix products, arithmetic and copies ran while one was open for 6% of the time, Pallas kernels for 0%

commit v1 on v0

v1 whole, which is shorter than its diff:
```python
import functools
import math

import jax
import jax.numpy as jnp
from jax import lax
from jax.experimental import pallas as pl
from jax.experimental.pallas import tpu as pltpu
from jax.sharding import PartitionSpec as P

HEAD_SIZE = 128
HEADS = 5
ITERS = 2
TOK = 128
ROWS = 256
QUART = 1280
WIDTH = 5120
HW = 640
SHARD = 160
HALF = 80
MESH = pl.DeviceIdType.MESH
F32 = jnp.float32
BF16 = jnp.bfloat16
N_MSG = 36


def kernel(
    lat_ref, noise_ref, table_ref, wq_ref, wk_ref, wv_ref, wo_ref, feats_ref, hg_ref, off_ref,
    out_ref,
    w, cur, y, acc, qkv, heads, part, rs_d2, rs_fin, t, x0, nz, mods, stat,
    tf, px_s, px_r, p1_s, p1_r, p2_s, p2_r, pe_s, pe_r, pfx, sl_s, sl_r,
    loc_sem, w_ss, w_rs, ag_ss, ag_rs, rs_ss, rs_rs, px_ss, px_rs,
):
    tm = lax.axis_index("tm")
    x = lax.axis_index("tp")
    core = lax.rem(tm, 2)
    chip = lax.div(tm, 2)
    yy, zz = lax.div(chip, 4), lax.rem(chip, 4)
    is0 = core == 0
    a = jnp.where(is0, zz, yy)
    b = jnp.where(is0, yy, zz)

    def rank(da, db):
        aa, bb = lax.rem(a + da, 4), lax.rem(b + db, 4)
        return jnp.where(is0, bb * 4 + aa, aa * 4 + bb) * 2 + core

    def dev(da, db):
        return (rank(da, db), x)

    sib = (tm + 1 - 2 * core, x)
    xp = (tm, lax.rem(x + 1, 4))
    xm = (tm, lax.rem(x + 3, 4))
    following = (lax.rem(tm + 1, 32), x)
    before = (lax.rem(tm + 31, 32), x)
    x1, x2, x3 = lax.rem(x + 1, 4), lax.rem(x + 2, 4), lax.rem(x + 3, 4)

    def remote(src, dst, ss, rs, to):
        return pltpu.make_async_remote_copy(
            src_ref=src, dst_ref=dst, send_sem=ss, recv_sem=rs, device_id=to, device_id_type=MESH
        )

    own = pl.ds(pl.multiple_of(SHARD * tm, 16), SHARD)
    local = [
        pltpu.make_async_copy(src, w.at[k, own], loc_sem.at[k])
        for k, src in enumerate((wq_ref, wk_ref, wv_ref, wo_ref))
    ]
    local.append(pltpu.make_async_copy(lat_ref, cur.at[0, x], loc_sem.at[4]))
    local.append(pltpu.make_async_copy(noise_ref, nz, loc_sem.at[5]))
    for c in local:
        c.start()

    barrier = pltpu.get_barrier_semaphore()
    peers = [sib, xp, xm, following, before]
    peers += [dev(k, 0) for k in (1, 2, 3)] + [dev(0, k) for k in (1, 2, 3)]
    for peer in peers:
        pl.semaphore_signal(barrier, inc=1, device_id=peer, device_id_type=MESH)
    pl.semaphore_wait(barrier, len(peers))

    for c in local:
        c.wait()

    def ag_msg(it, m):
        to = xp if m in (0, 2, 4) else xm
        src = (x, x, x, x, x3, x1)[m]
        step = (0, 1, 1, 0, 0, 1)[m]
        ref = cur.at[it, src, pl.ds(TOK * step, TOK)]
        return remote(ref, ref, ag_ss.at[it, m], ag_rs.at[it, m], to)

    def ag_start(it):
        for m in range(4):
            ag_msg(it, m).start()

    def ag_forward(it):
        ag_msg(it, 0).wait_recv()
        ag_msg(it, 4).start()
        ag_msg(it, 1).wait_recv()
        ag_msg(it, 5).start()

    def ag_finish(it):
        for m in (2, 3, 4, 5):
            ag_msg(it, m).wait_recv()
        for m in range(6):
            ag_msg(it, m).wait_send()

    def rows_of(r, lo, n):
        return pl.ds(pl.multiple_of(SHARD * r + lo, 16), n)

    def w_msg(k, m):
        if m < 4:
            ref = (
                w.at[k, rows_of(tm, 0, SHARD)],
                w.at[k, rows_of(tm, 0, SHARD)],
                w.at[k, rows_of(rank(3, 0), 0, HALF)],
                w.at[k, rows_of(rank(1, 0), HALF, HALF)],
            )[m]
            to = dev(1, 0) if m in (0, 2) else dev(3, 0)
        elif m < 20:
            j, i = divmod(m - 4, 4)
            da = (0, 3, 1, 2)[j]
            ref = (
                w.at[k, rows_of(rank(da, 0), 0, SHARD)],
                w.at[k, rows_of(rank(da, 0), 0, SHARD)],
                w.at[k, rows_of(rank(da, 3), 0, HALF)],
                w.at[k, rows_of(rank(da, 1), HALF, HALF)],
            )[i]
            to = dev(0, 1) if i in (0, 2) else dev(0, 3)
        else:
            j, i = divmod(m - 20, 4)
            ref = w.at[k, rows_of(rank((0, 3, 1, 2)[j], (0, 3, 1, 2)[i]), 0, SHARD)]
            to = sib
        return remote(ref, ref, w_ss.at[k, m], w_rs.at[k, m], to)

    def w_start(k, *ms):
        for m in ms:
            w_msg(k, m).start()

    def w_recv(k, *ms):
        for m in ms:
            w_msg(k, m).wait_recv()

    def s0(k):
        w_start(k, 0, 1, 4, 5, 20)

    def s1(k):
        w_recv(k, 0)
        w_start(k, 2, 8, 9, 24)
        w_recv(k, 1)
        w_start(k, 3, 12, 13, 28)

    def s2(k):
        w_recv(k, 2, 3)
        w_start(k, 16, 17, 32)

    def s3(k):
        for j in range(4):
            w_recv(k, 4 + 4 * j)
            w_start(k, 6 + 4 * j, 21 + 4 * j)
            w_recv(k, 5 + 4 * j)
            w_start(k, 7 + 4 * j, 22 + 4 * j)

    def s5(k):
        for j in range(4):
            w_recv(k, 6 + 4 * j, 7 + 4 * j)
            w_start(k, 23 + 4 * j)

    def s6(k):
        for m in range(20, 36):
            w_msg(k, m).wait_recv()

    def w_sent(k):
        for m in range(N_MSG):
            w_msg(k, m).wait_send()

    def modulation():
        for base in (0, 4, 8):
            count = 4 if base < 8 else 1
            for k in range(count):
                start = (base + k) * QUART if base < 8 else 2 * WIDTH + x * QUART
                pltpu.make_async_copy(
                    table_ref.at[:, pl.ds(pl.multiple_of(start, 128), QUART)],
                    part.at[k], loc_sem.at[k],
                ).start()
            for k in range(count):
                pltpu.make_async_copy(
                    table_ref.at[:, pl.ds(0, QUART)], part.at[k], loc_sem.at[k]
                ).wait()
                mods[base + k] = jnp.dot(feats_ref[...], part[k], preferred_element_type=F32)

    def norm(it):
        def body(i, carry):
            rows = pl.ds(pl.multiple_of(16 * i, 16), 16)
            step = lax.div(i, 8)
            total = jnp.zeros((16, 1), F32)
            for q in range(4):
                total += jnp.sum(cur[it, q, rows].astype(F32), axis=-1, keepdims=True)
            mean = total / WIDTH
            square = jnp.zeros((16, 1), F32)
            for q in range(4):
                d = cur[it, q, rows].astype(F32) - mean
                square += jnp.sum(d * d, axis=-1, keepdims=True)
            inv = lax.rsqrt(square / WIDTH + 1e-6)
            for q in range(4):
                d = (cur[it, q, rows].astype(F32) - mean) * inv
                shift = mods[q, pl.ds(step, 1)]
                scale = mods[4 + q, pl.ds(step, 1)]
                y[q, rows] = (d * (1.0 + scale) + shift).astype(BF16)
            return carry

        lax.fori_loop(0, 16, body, 0)

    def project(k):
        def body(q, carry):
            rows = pl.ds(pl.multiple_of(q * QUART, 128), QUART)
            acc[...] += jnp.dot(y[q], w[k, rows], preferred_element_type=F32)
            return carry

        acc[...] = jnp.zeros_like(acc)
        lax.fori_loop(0, 4, body, 0)
        qkv[k] = acc[...].astype(BF16)

    def attention():
        for step in range(2):
            for h in range(HEADS):
                rows, cols = pl.ds(TOK * step, TOK), pl.ds(HEAD_SIZE * h, HEAD_SIZE)
                s = lax.dot_general(
                    qkv[0, rows, cols], qkv[1, rows, cols], (((1,), (1,)), ((), ())),
                    preferred_element_type=F32,
                ) * (1.0 / math.sqrt(HEAD_SIZE))
                e = jnp.exp(s - jnp.max(s, axis=-1, keepdims=True))
                p = (e / jnp.sum(e, axis=-1, keepdims=True)).astype(BF16)
                heads[rows, cols] = jnp.dot(
                    p, qkv[2, rows, cols], preferred_element_type=F32
                ).astype(BF16)

    def out_part(q):
        def body(i, carry):
            rows = pl.ds(pl.multiple_of(q * QUART + i * 256, 128), 256)
            cols = pl.ds(pl.multiple_of(i * 256, 128), 256)
            part[q, :, cols] = lax.dot_general(
                heads[...], w[3, rows], (((1,), (1,)), ((), ())), preferred_element_type=F32
            ).astype(BF16)
            return carry

        lax.fori_loop(0, 5, body, 0)

    def rs_msg(it, m):
        step = (0, 1, 1, 0, 0, 1)[m]
        to = xp if m in (0, 2, 4) else xm
        rows = pl.ds(TOK * step, TOK)
        if m < 2:
            src, dst = part.at[x2, rows], rs_d2.at[it, m]
        elif m in (2, 4):
            src, dst = part.at[x1, rows], rs_fin.at[it, 0, rows]
        else:
            src, dst = part.at[x3, rows], rs_fin.at[it, 1, rows]
        return remote(src, dst, rs_ss.at[it, m], rs_rs.at[it, m], to)

    def add_in(it, m, q):
        step = (0, 1)[m]

        def body(i, carry):
            rows = pl.ds(pl.multiple_of(TOK * step + 16 * i, 16), 16)
            there = pl.ds(pl.multiple_of(16 * i, 16), 16)
            part[q, rows] = (part[q, rows].astype(F32) + rs_d2[it, m, there].astype(F32)).astype(BF16)
            return carry

        lax.fori_loop(0, 8, body, 0)

    def reduce_out(it):
        out_part(x2)
        rs_msg(it, 0).start()
        rs_msg(it, 1).start()
        out_part(x1)
        rs_msg(it, 2).start()
        out_part(x3)
        rs_msg(it, 3).start()
        rs_msg(it, 0).wait_recv()
        add_in(it, 0, x1)
        rs_msg(it, 4).start()
        rs_msg(it, 1).wait_recv()
        add_in(it, 1, x3)
        rs_msg(it, 5).start()
        out_part(x)
        for m in (2, 3, 4, 5):
            rs_msg(it, m).wait_recv()
        for m in range(6):
            rs_msg(it, m).wait_send()

    first = jnp.where(tm == 0, 1.0, 0.0).astype(F32)

    def terms(it):
        def body(i, carry):
            rows = pl.ds(pl.multiple_of(16 * i, 16), 16)
            step = lax.div(i, 8)
            attn = (
                part[x, rows].astype(F32)
                + rs_fin[it, 0, rows].astype(F32)
                + rs_fin[it, 1, rows].astype(F32)
            )
            gate = mods[8, pl.ds(step, 1)] * hg_ref[step]
            t[rows] = gate * attn + hg_ref[2 + step] * nz[rows].astype(F32)
            return carry

        lax.fori_loop(0, 16, body, 0)

        def body2(i, carry):
            rows = pl.ds(pl.multiple_of(16 * i, 16), 16)
            rows1 = pl.ds(pl.multiple_of(TOK + 16 * i, 16), 16)
            tf[rows] = t[rows] + t[rows1] + first * cur[0, x, rows].astype(F32)
            return carry

        lax.fori_loop(0, 8, body2, 0)

    mine = pl.ds(pl.multiple_of(64 * core, 64), 64)
    other = pl.ds(pl.multiple_of(64 - 64 * core, 64), 64)
    on0 = jnp.where(is0, 1.0, 0.0).astype(F32)
    on1 = 1.0 - on0

    def px_msg(it, m):
        if m == 0:
            src, dst, to = px_s, px_r.at[it], sib
        elif m < 4:
            src, dst, to = p1_s, p1_r.at[it, m - 1], dev(m, 0)
        elif m < 7:
            src, dst, to = p2_s.at[m - 4], p2_r.at[it, m - 4], dev(0, m - 3)
        elif m == 7:
            src, dst, to = pe_s, pe_r.at[it], sib
        else:
            src, dst, to = sl_s, sl_r, before
        return remote(src, dst, px_ss.at[it, m], px_rs.at[it, m], to)

    def prefix(it):
        px_s[...] = tf[other].astype(BF16)
        px_msg(it, 0).start()
        if it == ITERS - 1:
            sl_s[...] = t[0:TOK].astype(BF16)
            px_msg(it, 8).start()
        px_msg(it, 0).wait_recv()

        def loop(f):
            def body(i, carry):
                f(pl.ds(pl.multiple_of(16 * i, 16), 16),
                  pl.ds(pl.multiple_of(64 * core + 16 * i, 16), 16))
                return carry

            lax.fori_loop(0, 4, body, 0)

        def one(r, m):
            p1_s[r] = (tf[m] + px_r[it, r].astype(F32)).astype(BF16)

        loop(one)
        for k in (1, 3, 2):
            px_msg(it, k).start()
        for k in (1, 3, 2):
            px_msg(it, k).wait_recv()

        def two(r, m):
            chip_sum = tf[m] + px_r[it, r].astype(F32)
            lower = jnp.zeros((16, QUART), F32)
            total = chip_sum
            for k in (1, 2, 3):
                there = p1_r[it, k - 1, r].astype(F32)
                total += there
                lower += jnp.where(k <= a, 1.0, 0.0).astype(F32) * there
            pfx[m] = lower
            for k in (1, 2, 3):
                up = jnp.where(b + k < 4, 1.0, 0.0).astype(F32)
                p2_s[k - 1, r] = (on0 * total + on1 * (lower + up * chip_sum)).astype(BF16)

        loop(two)
        for k in (4, 6, 5):
            px_msg(it, k).start()
        for k in (4, 6, 5):
            px_msg(it, k).wait_recv()

        def three(r, m):
            p = pfx[m]
            for k in (1, 2, 3):
                keep = jnp.where(is0 & (k > b), 0.0, 1.0).astype(F32)
                p += keep * p2_r[it, k - 1, r].astype(F32)
            pe_s[r] = (p + on0 * tf[m]).astype(BF16)
            pfx[m] = p + on1 * px_r[it, r].astype(F32)

        loop(three)
        px_msg(it, 7).start()
        px_msg(it, 7).wait_recv()
        pfx[other] = pe_r[it].astype(F32)
        for m in range(8 + (it == ITERS - 1)):
            px_msg(it, m).wait_send()

    def advance(it):
        def body(i, carry):
            rows = pl.ds(pl.multiple_of(16 * i, 16), 16)
            rows1 = pl.ds(pl.multiple_of(TOK + 16 * i, 16), 16)
            p = pfx[rows] + first * cur[0, x, rows].astype(F32)
            cur[it + 1, x, rows] = p.astype(BF16)
            cur[it + 1, x, rows1] = (p + t[rows]).astype(BF16)
            return carry

        lax.fori_loop(0, 8, body, 0)

    def slide():
        px_msg(ITERS - 1, 8).wait_recv()
        one = off_ref[0] == 1
        last = tm == 31

        def body(i, carry):
            rows = pl.ds(pl.multiple_of(16 * i, 16), 16)
            rows1 = pl.ds(pl.multiple_of(TOK + 16 * i, 16), 16)
            c1 = pfx[rows] + first * cur[0, x, rows].astype(F32) + t[rows]
            c2 = c1 + t[rows1]
            c3 = c2 + sl_r[rows].astype(F32)
            c2 = jnp.where(last, c1, c2)
            c3 = jnp.where(last, c1, c3)
            out_ref[rows] = jnp.where(one, c1, c2).astype(BF16)
            out_ref[rows1] = jnp.where(one, c2, c3).astype(BF16)
            return carry

        lax.fori_loop(0, 8, body, 0)

    ag_start(0)
    for k in range(4):
        s0(k)
    s1(0)
    s2(0)
    ag_forward(0)
    modulation()
    s1(1)
    s2(1)
    ag_finish(0)
    norm(0)

    def weights(k, carry):
        s3(k)

        @pl.when(k < 2)
        def _():
            s1(k + 2)
            s2(k + 2)

        s5(k)
        s6(k)
        project(k)
        return carry

    lax.fori_loop(0, 3, weights, 0)
    attention()
    s3(3)
    s5(3)
    s6(3)
    reduce_out(0)
    terms(0)
    prefix(0)
    advance(0)
    lax.fori_loop(0, 4, lambda k, c: (w_sent(k), c)[1], 0)

    ag_start(1)
    ag_forward(1)
    ag_finish(1)
    norm(1)
    lax.fori_loop(0, 3, lambda k, c: (project(k), c)[1], 0)
    attention()
    reduce_out(1)
    terms(1)
    prefix(1)
    slide()


def features(step_index, mod_table):
    half = mod_table.shape[0] // 2
    freqs = jnp.exp(-math.log(10000.0) * jnp.arange(half).astype(F32) / half)
    angles = step_index.astype(F32)[:, None] * freqs[None, :]
    return jnp.concatenate([jnp.cos(angles), jnp.sin(angles)], axis=1).astype(BF16)


def per_device(latents, noise, mod_table, w_query, w_key, w_value, w_out, step_index, slide_offset):
    feats = features(step_index, mod_table)
    feats = jnp.concatenate([feats, jnp.zeros((14, feats.shape[1]), BF16)], axis=0)
    step_size = (step_index.astype(F32) + 1.0) / 2000.0
    hg = jnp.concatenate([step_size, 0.2 * jnp.sqrt(step_size)])
    hbm = pl.BlockSpec(memory_space=pl.ANY)
    vmem = pl.BlockSpec(memory_space=pltpu.VMEM)
    smem = pl.BlockSpec(memory_space=pltpu.SMEM)
    dma = pltpu.SemaphoreType.DMA
    out = pl.pallas_call(
        kernel,
        out_shape=jax.ShapeDtypeStruct((ROWS, QUART), BF16),
        in_specs=[hbm] * 7 + [vmem, smem, smem],
        out_specs=vmem,
        scratch_shapes=[
            pltpu.VMEM((4, WIDTH, HW), BF16),
            pltpu.VMEM((ITERS, 4, ROWS, QUART), BF16),
            pltpu.VMEM((4, ROWS, QUART), BF16),
            pltpu.VMEM((ROWS, HW), F32),
            pltpu.VMEM((3, ROWS, HW), BF16),
            pltpu.VMEM((ROWS, HW), BF16),
            pltpu.VMEM((4, ROWS, QUART), BF16),
            pltpu.VMEM((ITERS, 2, TOK, QUART), BF16),
            pltpu.VMEM((ITERS, 2, ROWS, QUART), BF16),
            pltpu.VMEM((ROWS, QUART), F32),
            pltpu.VMEM((16, 128), BF16),
            pltpu.VMEM((ROWS, QUART), BF16),
            pltpu.VMEM((9, 16, QUART), F32),
            pltpu.VMEM((8, 128), F32),
            pltpu.VMEM((TOK, QUART), F32),
            pltpu.VMEM((64, QUART), BF16),
            pltpu.VMEM((ITERS, 64, QUART), BF16),
            pltpu.VMEM((64, QUART), BF16),
            pltpu.VMEM((ITERS, 3, 64, QUART), BF16),
            pltpu.VMEM((3, 64, QUART), BF16),
            pltpu.VMEM((ITERS, 3, 64, QUART), BF16),
            pltpu.VMEM((64, QUART), BF16),
            pltpu.VMEM((ITERS, 64, QUART), BF16),
            pltpu.VMEM((TOK, QUART), F32),
            pltpu.VMEM((TOK, QUART), BF16),
            pltpu.VMEM((TOK, QUART), BF16),
            dma((6,)),
            dma((4, N_MSG)),
            dma((4, N_MSG)),
            dma((ITERS, 6)),
            dma((ITERS, 6)),
            dma((ITERS, 6)),
            dma((ITERS, 6)),
            dma((ITERS, 9)),
            dma((ITERS, 9)),
        ],
        compiler_params=pltpu.CompilerParams(
            collective_id=0, has_side_effects=True, vmem_limit_bytes=62 * 1024 * 1024
        ),
        cost_estimate=pl.CostEstimate(
            flops=2 * ITERS * 4 * ROWS * WIDTH * HW, bytes_accessed=12_000_000, transcendentals=0
        ),
    )(
        latents.reshape(ROWS, QUART), noise.reshape(ROWS, QUART), mod_table,
        w_query, w_key, w_value, w_out.T, feats, hg, slide_offset.reshape(1),
    )
    return out.reshape(latents.shape)


def solution(mesh):
    placed = (
        P("tm", None, "tp"),
        P("tm", None, "tp"),
        P(),
        P("tm", "tp"),
        P("tm", "tp"),
        P("tm", "tp"),
        P("tp", "tm"),
        P("tm"),
        P(),
    )
    return jax.shard_map(
        per_device, mesh=mesh, in_specs=placed, out_specs=P("tm", None, "tp"), check_vma=False
    )
```

time: 632 us -> 229 us (0.36)
  waiting for transfers between devices: 434 us -> 0 us
  Pallas kernels: 0 us -> 222 us
  other arithmetic: 104 us -> 2.67 us
  matrix products: 61.4 us -> 0 us
  between operations: 14.4 us -> 0.67 us
  local copies, waits for them, and re-layouts: 10.5 us -> 1.97 us
    all_gather x8 -> x0, waiting for transfers between devices: 356 us -> none  [the longest x2 116 us: prefix_2(): everything = lax.all_gather(x.astype(jnp.bfloat16), axis)]
    pallas_call x0 -> x1, Pallas kernels: none -> 222 us  [per_device(): pl.pallas_call(kernel, out_shape=jax.ShapeDtypeStruct((ROWS, QUART), BF16...]
    select_n x65 -> x0, other arithmetic: 84 us -> none  [the longest x64 83.9 us: step(): return jnp.where(reached, new, before)]
    reduce_scatter x2 -> x0, waiting for transfers between devices: 66.5 us -> none  [per_device(): lax.psum_scatter(partial_value.astype(jnp.bfloat16), 'tp', scatter_dimens...]
    dot_general x13 -> x0, matrix products: 58.3 us -> none  [the longest x2 13.4 us: attention_part(): jnp.dot(head_outputs, full_out, preferred_element_type=jnp.float32)]
    reshape x6 -> x0, local copies, waits for them, and re-layouts: 10.5 us -> none  [the longest x2 4.28 us: attention_part(): key_rows = jnp.dot(inputs, full_key, preferred_element_type=jnp.float32)....]
    reduce_sum x4 -> x0, other arithmetic: 9.79 us -> none  [the longest x2 5.14 us: attention_part(): var = jnp.mean(centred * centred, axis=-1, keepdims=True)]
    ppermute x1 -> x0, waiting for transfers between devices: 9.05 us -> none  [passed_along(): return lax.ppermute(block, axis, route)]
  transfers between devices with their start and end apart: 11 -> 0, of which waited for: 11 -> 0; matrix products, arithmetic and copies ran while one was open for 6% -> 0% of each run, Pallas kernels for 0% -> 0%
where the time goes in v1:
time: 229 us; the launch traced here: 227 us
  Pallas kernels  222 us (97%)
  other arithmetic  2.67 us (1%)
    pallas_call x1, Pallas kernels, per_device(): pl.pallas_call(kernel, out_shape=jax.ShapeDtypeStruct((ROWS, QUART), BF16...  222 us

profile of v1, /device:TPU:1, one launch (start us, length us, event | category | flops | bytes accessed | tf_op | source)
XLA Modules:
  0.0 227.4 jit_solution(8817500775444756058)
XLA Ops:
  0.7 0.7 convert_element_type.12
  1.3 0.1 fusion.3
  1.4 0.7 add_multiply_fusion
  2.1 0.6 pad_maximum_fusion.hg_ref
  2.7 0.6 fusion.2.feats_ref
  3.3 222.1 %shard_map.91 = bf16[256,1280]{1,0:T(8,128)(2,1)} custom-call(bf16[256,1280]{1,0:T(8,128)(2,1)} %bitcast.7, bf16[256,1280]{1,0:T(8,128)(2,1)} %bitcast.8, bf16[256,15360]{1,0:T(8,128)(2,1)} %table_ref.1, bf16[160,640]{1,0:T(8,128)(2,1)} %wq_ref.1, bf16[160,640]{1,0:T(8,128)(2,1)} %wk_ref.1, bf16[160,640]{1,0:T(8,128)(2,1)} %wv_ref.1, ...), custom_call_target="tpu_custom_call" | custom-call | flops 13421772800 | bytes 12000000 | tf_op jit(solution)/shard_map/pallas_call | solution.py:485
  225.5 2.0 copy.12
  (1 shorter events, 0.0 us)

commit v2 on v1

--- a/solution.py
+++ b/solution.py
@@ -27,9 +27,9 @@
 def kernel(
     lat_ref, noise_ref, table_ref, wq_ref, wk_ref, wv_ref, wo_ref, feats_ref, hg_ref, off_ref,
     out_ref,
-    w, cur, y, acc, qkv, heads, part, rs_d2, rs_fin, t, x0, nz, mods, stat,
+    w, cur, y, acc, qkv, hd, part, tb, t, nz, mods, stat,
     tf, px_s, px_r, p1_s, p1_r, p2_s, p2_r, pe_s, pe_r, pfx, sl_s, sl_r,
-    loc_sem, w_ss, w_rs, ag_ss, ag_rs, rs_ss, rs_rs, px_ss, px_rs,
+    loc_sem, w_ss, w_rs, ag_ss, ag_rs, hd_ss, hd_rs, px_ss, px_rs, tr_ss, tr_rs,
 ):
     tm = lax.axis_index("tm")
     x = lax.axis_index("tp")
@@ -52,6 +52,8 @@
     xm = (tm, lax.rem(x + 3, 4))
     following = (lax.rem(tm + 1, 32), x)
     before = (lax.rem(tm + 31, 32), x)
+    swapped = ((x * 4 + zz) * 2 + core, yy)
+    swaps = x != yy
     x1, x2, x3 = lax.rem(x + 1, 4), lax.rem(x + 2, 4), lax.rem(x + 3, 4)
 
     def remote(src, dst, ss, rs, to):
@@ -62,7 +64,7 @@
     own = pl.ds(pl.multiple_of(SHARD * tm, 16), SHARD)
     local = [
         pltpu.make_async_copy(src, w.at[k, own], loc_sem.at[k])
-        for k, src in enumerate((wq_ref, wk_ref, wv_ref, wo_ref))
+        for k, src in enumerate((wq_ref, wk_ref, wv_ref))
     ]
     local.append(pltpu.make_async_copy(lat_ref, cur.at[0, x], loc_sem.at[4]))
     local.append(pltpu.make_async_copy(noise_ref, nz, loc_sem.at[5]))
@@ -74,33 +76,86 @@
     peers += [dev(k, 0) for k in (1, 2, 3)] + [dev(0, k) for k in (1, 2, 3)]
     for peer in peers:
         pl.semaphore_signal(barrier, inc=1, device_id=peer, device_id_type=MESH)
-    pl.semaphore_wait(barrier, len(peers))
+
+    @pl.when(swaps)
+    def _():
+        pl.semaphore_signal(barrier, inc=1, device_id=swapped, device_id_type=MESH)
+
+    pl.semaphore_wait(barrier, len(peers) + jnp.where(swaps, 1, 0))
+
+    def swap_msg():
+        there = pl.ds(pl.multiple_of(SHARD * swapped[0], 16), SHARD)
+        return remote(wo_ref, w.at[3, there], tr_ss, tr_rs, swapped)
+
+    def swap_local():
+        return pltpu.make_async_copy(wo_ref, w.at[3, own], loc_sem.at[3])
+
+    @pl.when(swaps)
+    def _():
+        swap_msg().start()
+
+    @pl.when(jnp.logical_not(swaps))
+    def _():
+        swap_local().start()
+
+    def swap_finish():
+        @pl.when(swaps)
+        def _():
+            swap_msg().wait()
+
+        @pl.when(jnp.logical_not(swaps))
+        def _():
+            swap_local().wait()
 
     for c in local:
         c.wait()
 
-    def ag_msg(it, m):
-        to = xp if m in (0, 2, 4) else xm
-        src = (x, x, x, x, x3, x1)[m]
-        step = (0, 1, 1, 0, 0, 1)[m]
-        ref = cur.at[it, src, pl.ds(TOK * step, TOK)]
-        return remote(ref, ref, ag_ss.at[it, m], ag_rs.at[it, m], to)
-
-    def ag_start(it):
-        for m in range(4):
-            ag_msg(it, m).start()
-
-    def ag_forward(it):
-        ag_msg(it, 0).wait_recv()
-        ag_msg(it, 4).start()
-        ag_msg(it, 1).wait_recv()
-        ag_msg(it, 5).start()
-
-    def ag_finish(it):
-        for m in (2, 3, 4, 5):
-            ag_msg(it, m).wait_recv()
-        for m in range(6):
-            ag_msg(it, m).wait_send()
+    class Gather:
+        def __init__(self, block, halves, ss, rs):
+            self.block, self.halves, self.ss, self.rs = block, halves, ss, rs
+
+        def msg(self, m):
+            to = xp if m in (0, 2, 4) else xm
+            src = (x, x, x, x, x3, x1)[m]
+            ref = self.block(src, self.halves[(0, 1, 1, 0, 0, 1)[m]])
+            return remote(ref, ref, self.ss(m), self.rs(m), to)
+
+        def start(self, *ms):
+            for m in ms:
+                self.msg(m).start()
+
+        def forward(self):
+            self.msg(0).wait_recv()
+            self.msg(4).start()
+            self.msg(1).wait_recv()
+            self.msg(5).start()
+
+        def recv(self, *ms):
+            for m in ms:
+                self.msg(m).wait_recv()
+
+        def sent(self):
+            for m in range(6):
+                self.msg(m).wait_send()
+
+    steps = (pl.ds(0, TOK), pl.ds(TOK, TOK))
+    lat_g = Gather(lambda q, r: cur.at[0, q, r], steps, lambda m: ag_ss.at[0, m], lambda m: ag_rs.at[0, m])
+    t0_g = Gather(
+        lambda q, r: tb.at[q, r], (pl.ds(0, 64), pl.ds(64, 64)),
+        lambda m: ag_ss.at[1, m], lambda m: ag_rs.at[1, m],
+    )
+    pfx_g = Gather(
+        lambda q, r: cur.at[1, q, r],
+        (pl.ds(pl.multiple_of(64 * core, 64), 64), pl.ds(pl.multiple_of(64 - 64 * core, 64), 64)),
+        lambda m: ag_ss.at[2, m], lambda m: ag_rs.at[2, m],
+    )
+    hd_g = [
+        Gather(
+            lambda q, r, it=it: hd.at[it, q, r], steps,
+            lambda m, it=it: hd_ss.at[it, m], lambda m, it=it: hd_rs.at[it, m],
+        )
+        for it in range(ITERS)
+    ]
 
     def rows_of(r, lo, n):
         return pl.ds(pl.multiple_of(SHARD * r + lo, 16), n)
@@ -186,18 +241,37 @@
                 ).wait()
                 mods[base + k] = jnp.dot(feats_ref[...], part[k], preferred_element_type=F32)
 
+    def block_stats(it, q):
+        def body(i, carry):
+            rows = pl.ds(pl.multiple_of(16 * i, 16), 16)
+            c = cur[it, q, rows].astype(F32)
+            mean = jnp.sum(c, axis=-1, keepdims=True) / QUART
+            d = c - mean
+            stat[q, 0, rows] = jnp.broadcast_to(mean, (16, 128))
+            stat[q, 1, rows] = jnp.broadcast_to(jnp.sum(d * d, axis=-1, keepdims=True), (16, 128))
+            return carry
+
+        lax.fori_loop(0, 16, body, 0)
+
+    def block_second(q):
+        def body(i, carry):
+            rows = pl.ds(pl.multiple_of(16 * i, 16), 16)
+            rows1 = pl.ds(pl.multiple_of(TOK + 16 * i, 16), 16)
+            cur[1, q, rows1] = (cur[1, q, rows].astype(F32) + tb[q, rows].astype(F32)).astype(BF16)
+            return carry
+
+        lax.fori_loop(0, 8, body, 0)
+
     def norm(it):
         def body(i, carry):
             rows = pl.ds(pl.multiple_of(16 * i, 16), 16)
             step = lax.div(i, 8)
-            total = jnp.zeros((16, 1), F32)
-            for q in range(4):
-                total += jnp.sum(cur[it, q, rows].astype(F32), axis=-1, keepdims=True)
-            mean = total / WIDTH
+            means = [stat[q, 0, rows][:, :1] for q in range(4)]
+            mean = (means[0] + means[1] + means[2] + means[3]) * 0.25
             square = jnp.zeros((16, 1), F32)
             for q in range(4):
-                d = cur[it, q, rows].astype(F32) - mean
-                square += jnp.sum(d * d, axis=-1, keepdims=True)
+                off = means[q] - mean
+                square += stat[q, 1, rows][:, :1] + QUART * off * off
             inv = lax.rsqrt(square / WIDTH + 1e-6)
             for q in range(4):
                 d = (cur[it, q, rows].astype(F32) - mean) * inv
@@ -218,7 +292,7 @@
         lax.fori_loop(0, 4, body, 0)
         qkv[k] = acc[...].astype(BF16)
 
-    def attention():
+    def attention(it):
         for step in range(2):
             for h in range(HEADS):
                 rows, cols = pl.ds(TOK * step, TOK), pl.ds(HEAD_SIZE * h, HEAD_SIZE)
@@ -228,63 +302,35 @@
                 ) * (1.0 / math.sqrt(HEAD_SIZE))
                 e = jnp.exp(s - jnp.max(s, axis=-1, keepdims=True))
                 p = (e / jnp.sum(e, axis=-1, keepdims=True)).astype(BF16)
-                heads[rows, cols] = jnp.dot(
+                hd[it, x, rows, cols] = jnp.dot(
                     p, qkv[2, rows, cols], preferred_element_type=F32
                 ).astype(BF16)
-
-    def out_part(q):
+            if step == 0:
+                hd_g[it].start(0, 3)
+            else:
+                hd_g[it].start(1, 2)
+
+    def out_part(it, q, add):
         def body(i, carry):
             rows = pl.ds(pl.multiple_of(q * QUART + i * 256, 128), 256)
             cols = pl.ds(pl.multiple_of(i * 256, 128), 256)
-            part[q, :, cols] = lax.dot_general(
-                heads[...], w[3, rows], (((1,), (1,)), ((), ())), preferred_element_type=F32
-            ).astype(BF16)
+            new = lax.dot_general(
+                hd[it, q], w[3, rows], (((1,), (1,)), ((), ())), preferred_element_type=F32
+            )
+            t[:, cols] = t[:, cols] + new if add else new
             return carry
 
         lax.fori_loop(0, 5, body, 0)
 
-    def rs_msg(it, m):
-        step = (0, 1, 1, 0, 0, 1)[m]
-        to = xp if m in (0, 2, 4) else xm
-        rows = pl.ds(TOK * step, TOK)
-        if m < 2:
-            src, dst = part.at[x2, rows], rs_d2.at[it, m]
-        elif m in (2, 4):
-            src, dst = part.at[x1, rows], rs_fin.at[it, 0, rows]
-        else:
-            src, dst = part.at[x3, rows], rs_fin.at[it, 1, rows]
-        return remote(src, dst, rs_ss.at[it, m], rs_rs.at[it, m], to)
-
-    def add_in(it, m, q):
-        step = (0, 1)[m]
-
-        def body(i, carry):
-            rows = pl.ds(pl.multiple_of(TOK * step + 16 * i, 16), 16)
-            there = pl.ds(pl.multiple_of(16 * i, 16), 16)
-            part[q, rows] = (part[q, rows].astype(F32) + rs_d2[it, m, there].astype(F32)).astype(BF16)
-            return carry
-
-        lax.fori_loop(0, 8, body, 0)
-
-    def reduce_out(it):
-        out_part(x2)
-        rs_msg(it, 0).start()
-        rs_msg(it, 1).start()
-        out_part(x1)
-        rs_msg(it, 2).start()
-        out_part(x3)
-        rs_msg(it, 3).start()
-        rs_msg(it, 0).wait_recv()
-        add_in(it, 0, x1)
-        rs_msg(it, 4).start()
-        rs_msg(it, 1).wait_recv()
-        add_in(it, 1, x3)
-        rs_msg(it, 5).start()
-        out_part(x)
-        for m in (2, 3, 4, 5):
-            rs_msg(it, m).wait_recv()
-        for m in range(6):
-            rs_msg(it, m).wait_send()
+    def out_project(it):
+        g = hd_g[it]
+        out_part(it, x, False)
+        g.recv(2)
+        out_part(it, x3, True)
+        g.recv(3)
+        out_part(it, x1, True)
+        g.recv(4, 5)
+        out_part(it, x2, True)
 
     first = jnp.where(tm == 0, 1.0, 0.0).astype(F32)
 
@@ -292,13 +338,8 @@
         def body(i, carry):
             rows = pl.ds(pl.multiple_of(16 * i, 16), 16)
             step = lax.div(i, 8)
-            attn = (
-                part[x, rows].astype(F32)
-                + rs_fin[it, 0, rows].astype(F32)
-                + rs_fin[it, 1, rows].astype(F32)
-            )
             gate = mods[8, pl.ds(step, 1)] * hg_ref[step]
-            t[rows] = gate * attn + hg_ref[2 + step] * nz[rows].astype(F32)
+            t[rows] = gate * t[rows] + hg_ref[2 + step] * nz[rows].astype(F32)
             return carry
 
         lax.fori_loop(0, 16, body, 0)
@@ -306,7 +347,10 @@
         def body2(i, carry):
             rows = pl.ds(pl.multiple_of(16 * i, 16), 16)
             rows1 = pl.ds(pl.multiple_of(TOK + 16 * i, 16), 16)
-            tf[rows] = t[rows] + t[rows1] + first * cur[0, x, rows].astype(F32)
+            t0 = t[rows]
+            tf[rows] = t0 + t[rows1] + first * cur[0, x, rows].astype(F32)
+            if it == 0:
+                tb[x, rows] = t0.astype(BF16)
             return carry
 
         lax.fori_loop(0, 8, body2, 0)
@@ -353,6 +397,8 @@
             px_msg(it, k).start()
         for k in (1, 3, 2):
             px_msg(it, k).wait_recv()
+        if it == 0:
+            t0_g.forward()
 
         def two(r, m):
             chip_sum = tf[m] + px_r[it, r].astype(F32)
@@ -379,25 +425,29 @@
                 keep = jnp.where(is0 & (k > b), 0.0, 1.0).astype(F32)
                 p += keep * p2_r[it, k - 1, r].astype(F32)
             pe_s[r] = (p + on0 * tf[m]).astype(BF16)
-            pfx[m] = p + on1 * px_r[it, r].astype(F32)
+            p += on1 * px_r[it, r].astype(F32) + first * cur[0, x, m].astype(F32)
+            pfx[m] = p
+            if it == 0:
+                cur[1, x, m] = p.astype(BF16)
 
         loop(three)
         px_msg(it, 7).start()
+        if it == 0:
+            pfx_g.start(0, 3)
         px_msg(it, 7).wait_recv()
-        pfx[other] = pe_r[it].astype(F32)
+
+        def four(r, m):
+            there = pl.ds(pl.multiple_of(64 - 64 * core + r.start, 16), 16)
+            p = pe_r[it, r].astype(F32) + first * cur[0, x, there].astype(F32)
+            pfx[there] = p
+            if it == 0:
+                cur[1, x, there] = p.astype(BF16)
+
+        loop(four)
+        if it == 0:
+            pfx_g.start(2, 1)
         for m in range(8 + (it == ITERS - 1)):
             px_msg(it, m).wait_send()
-
-    def advance(it):
-        def body(i, carry):
-            rows = pl.ds(pl.multiple_of(16 * i, 16), 16)
-            rows1 = pl.ds(pl.multiple_of(TOK + 16 * i, 16), 16)
-            p = pfx[rows] + first * cur[0, x, rows].astype(F32)
-            cur[it + 1, x, rows] = p.astype(BF16)
-            cur[it + 1, x, rows1] = (p + t[rows]).astype(BF16)
-            return carry
-
-        lax.fori_loop(0, 8, body, 0)
 
     def slide():
         px_msg(ITERS - 1, 8).wait_recv()
@@ -407,7 +457,7 @@
         def body(i, carry):
             rows = pl.ds(pl.multiple_of(16 * i, 16), 16)
             rows1 = pl.ds(pl.multiple_of(TOK + 16 * i, 16), 16)
-            c1 = pfx[rows] + first * cur[0, x, rows].astype(F32) + t[rows]
+            c1 = pfx[rows] + t[rows]
             c2 = c1 + t[rows1]
             c3 = c2 + sl_r[rows].astype(F32)
             c2 = jnp.where(last, c1, c2)
@@ -418,16 +468,24 @@
 
         lax.fori_loop(0, 8, body, 0)
 
-    ag_start(0)
-    for k in range(4):
-        s0(k)
+    lat_g.start(0, 1, 2, 3)
+    s0(0)
+    s0(1)
+    s0(2)
     s1(0)
     s2(0)
-    ag_forward(0)
+    swap_finish()
+    s0(3)
+    lat_g.forward()
     modulation()
     s1(1)
     s2(1)
-    ag_finish(0)
+    block_stats(0, x)
+    lat_g.recv(2, 3)
+    block_stats(0, x1)
+    block_stats(0, x3)
+    lat_g.recv(4, 5)
+    block_stats(0, x2)
     norm(0)
 
     def weights(k, carry):
@@ -444,26 +502,40 @@
         return carry
 
     lax.fori_loop(0, 3, weights, 0)
-    attention()
+    attention(0)
     s3(3)
+    hd_g[0].forward()
     s5(3)
     s6(3)
-    reduce_out(0)
+    out_project(0)
     terms(0)
+    t0_g.start(0, 1, 2, 3)
     prefix(0)
-    advance(0)
     lax.fori_loop(0, 4, lambda k, c: (w_sent(k), c)[1], 0)
-
-    ag_start(1)
-    ag_forward(1)
-    ag_finish(1)
+    lat_g.sent()
+    hd_g[0].sent()
+    t0_g.recv(2, 3, 4, 5)
+    block_second(x)
+    block_stats(1, x)
+    pfx_g.forward()
+    pfx_g.recv(2, 3)
+    for q in (x1, x3):
+        block_second(q)
+        block_stats(1, q)
+    pfx_g.recv(4, 5)
+    block_second(x2)
+    block_stats(1, x2)
     norm(1)
     lax.fori_loop(0, 3, lambda k, c: (project(k), c)[1], 0)
-    attention()
-    reduce_out(1)
+    attention(1)
+    hd_g[1].forward()
+    out_project(1)
     terms(1)
     prefix(1)
     slide()
+    t0_g.sent()
+    pfx_g.sent()
+    hd_g[1].sent()
 
 
 def features(step_index, mod_table):
@@ -493,15 +565,13 @@
             pltpu.VMEM((4, ROWS, QUART), BF16),
             pltpu.VMEM((ROWS, HW), F32),
             pltpu.VMEM((3, ROWS, HW), BF16),
-            pltpu.VMEM((ROWS, HW), BF16),
+            pltpu.VMEM((ITERS, 4, ROWS, HW), BF16),
             pltpu.VMEM((4, ROWS, QUART), BF16),
-            pltpu.VMEM((ITERS, 2, TOK, QUART), BF16),
-            pltpu.VMEM((ITERS, 2, ROWS, QUART), BF16),
+            pltpu.VMEM((4, TOK, QUART), BF16),
             pltpu.VMEM((ROWS, QUART), F32),
-            pltpu.VMEM((16, 128), BF16),
             pltpu.VMEM((ROWS, QUART), BF16),
             pltpu.VMEM((9, 16, QUART), F32),
-            pltpu.VMEM((8, 128), F32),
+            pltpu.VMEM((4, 2, ROWS, 128), F32),
             pltpu.VMEM((TOK, QUART), F32),
             pltpu.VMEM((64, QUART), BF16),
             pltpu.VMEM((ITERS, 64, QUART), BF16),
@@ -517,12 +587,14 @@
             dma((6,)),
             dma((4, N_MSG)),
             dma((4, N_MSG)),
-            dma((ITERS, 6)),
-            dma((ITERS, 6)),
+            dma((3, 6)),
+            dma((3, 6)),
             dma((ITERS, 6)),
             dma((ITERS, 6)),
             dma((ITERS, 9)),
             dma((ITERS, 9)),
+            dma,
+            dma,
         ],
         compiler_params=pltpu.CompilerParams(
             collective_id=0, has_side_effects=True, vmem_limit_bytes=62 * 1024 * 1024

time: 229 us -> 198 us (0.86)
  Pallas kernels: 222 us -> 192 us
    pallas_call x1, Pallas kernels: 222 us -> 192 us  [per_device(): pl.pallas_call(kernel, out_shape=jax.ShapeDtypeStruct((ROWS, QUART), BF16...]
where the time goes in v2:
time: 198 us; the launch traced here: 197 us
  Pallas kernels  192 us (97%)
  other arithmetic  2.67 us (1%)
    pallas_call x1, Pallas kernels, per_device(): pl.pallas_call(kernel, out_shape=jax.ShapeDtypeStruct((ROWS, QUART), BF16...  192 us

profile of v2, /device:TPU:1, one launch (start us, length us, event | category | flops | bytes accessed | tf_op | source)
XLA Modules:
  0.0 197.2 jit_solution(2118133758513728407)
XLA Ops:
  0.7 0.7 convert_element_type.12
  1.3 0.1 fusion.3
  1.4 0.7 add_multiply_fusion
  2.1 0.6 pad_maximum_fusion.hg_ref
  2.7 0.6 fusion.2.feats_ref
  3.3 191.9 %shard_map.91 = bf16[256,1280]{1,0:T(8,128)(2,1)} custom-call(bf16[256,1280]{1,0:T(8,128)(2,1)} %bitcast.7, bf16[256,1280]{1,0:T(8,128)(2,1)} %bitcast.8, bf16[256,15360]{1,0:T(8,128)(2,1)} %table_ref.1, bf16[160,640]{1,0:T(8,128)(2,1)} %wq_ref.1, bf16[160,640]{1,0:T(8,128)(2,1)} %wk_ref.1, bf16[160,640]{1,0:T(8,128)(2,1)} %wv_ref.1, ...), custom_call_target="tpu_custom_call" | custom-call | flops 13421772800 | bytes 12000000 | tf_op jit(solution)/shard_map/pallas_call | solution.py:557
  195.2 2.0 copy.12
  (1 shorter events, 0.0 us)

commit v3 on v2

--- a/solution.py
+++ b/solution.py
@@ -25,9 +25,9 @@
 
 
 def kernel(
-    lat_ref, noise_ref, table_ref, wq_ref, wk_ref, wv_ref, wo_ref, feats_ref, hg_ref, off_ref,
+    lat_ref, noise_ref, table_ref, wq_ref, wk_ref, wv_ref, wo_ref, feats_ref, hg_ref,
     out_ref,
-    w, cur, y, acc, qkv, hd, part, tb, t, nz, mods, stat,
+    w, cur, y, acc, qkv, hda, hdb, part, tb, t, nz, mods, stat,
     tf, px_s, px_r, p1_s, p1_r, p2_s, p2_r, pe_s, pe_r, pfx, sl_s, sl_r,
     loc_sem, w_ss, w_rs, ag_ss, ag_rs, hd_ss, hd_rs, px_ss, px_rs, tr_ss, tr_rs,
 ):
@@ -88,15 +88,16 @@
         return remote(wo_ref, w.at[3, there], tr_ss, tr_rs, swapped)
 
     def swap_local():
-        return pltpu.make_async_copy(wo_ref, w.at[3, own], loc_sem.at[3])
-
-    @pl.when(swaps)
-    def _():
-        swap_msg().start()
-
-    @pl.when(jnp.logical_not(swaps))
-    def _():
-        swap_local().start()
+        return pltpu.make_async_copy(wo_ref, w.at[3, own], loc_sem.at[6])
+
+    def swap_start():
+        @pl.when(swaps)
+        def _():
+            swap_msg().start()
+
+        @pl.when(jnp.logical_not(swaps))
+        def _():
+            swap_local().start()
 
     def swap_finish():
         @pl.when(swaps)
@@ -149,13 +150,17 @@
         (pl.ds(pl.multiple_of(64 * core, 64), 64), pl.ds(pl.multiple_of(64 - 64 * core, 64), 64)),
         lambda m: ag_ss.at[2, m], lambda m: ag_rs.at[2, m],
     )
-    hd_g = [
-        Gather(
-            lambda q, r, it=it: hd.at[it, q, r], steps,
-            lambda m, it=it: hd_ss.at[it, m], lambda m, it=it: hd_rs.at[it, m],
+    hd = (hda, hdb)
+    blocks = (pl.ds(0, 256), pl.ds(256, 384))
+    block_heads = ((0, 1), (2, 3, 4))
+
+    def hd_gather(it, c):
+        return Gather(
+            lambda q, r: hd[c].at[it, q, r], steps,
+            lambda m: hd_ss.at[it, c, m], lambda m: hd_rs.at[it, c, m],
         )
-        for it in range(ITERS)
-    ]
+
+    hd_g = [[hd_gather(it, c) for c in range(2)] for it in range(ITERS)]
 
     def rows_of(r, lo, n):
         return pl.ds(pl.multiple_of(SHARD * r + lo, 16), n)
@@ -206,8 +211,8 @@
         w_recv(k, 2, 3)
         w_start(k, 16, 17, 32)
 
-    def s3(k):
-        for j in range(4):
+    def s3(k, parts=(0, 1, 2, 3)):
+        for j in parts:
             w_recv(k, 4 + 4 * j)
             w_start(k, 6 + 4 * j, 21 + 4 * j)
             w_recv(k, 5 + 4 * j)
@@ -243,15 +248,15 @@
 
     def block_stats(it, q):
         def body(i, carry):
-            rows = pl.ds(pl.multiple_of(16 * i, 16), 16)
+            rows = pl.ds(pl.multiple_of(32 * i, 32), 32)
             c = cur[it, q, rows].astype(F32)
             mean = jnp.sum(c, axis=-1, keepdims=True) / QUART
             d = c - mean
-            stat[q, 0, rows] = jnp.broadcast_to(mean, (16, 128))
-            stat[q, 1, rows] = jnp.broadcast_to(jnp.sum(d * d, axis=-1, keepdims=True), (16, 128))
-            return carry
-
-        lax.fori_loop(0, 16, body, 0)
+            stat[q, 0, rows] = jnp.broadcast_to(mean, (32, 128))
+            stat[q, 1, rows] = jnp.broadcast_to(jnp.sum(d * d, axis=-1, keepdims=True), (32, 128))
+            return carry
+
+        lax.fori_loop(0, 8, body, 0)
 
     def block_second(q):
         def body(i, carry):
@@ -264,23 +269,27 @@
 
     def norm(it):
         def body(i, carry):
-            rows = pl.ds(pl.multiple_of(16 * i, 16), 16)
-            step = lax.div(i, 8)
-            means = [stat[q, 0, rows][:, :1] for q in range(4)]
+            rows = pl.ds(pl.multiple_of(32 * i, 32), 32)
+            step = lax.div(i, 4)
+            means = [stat[q, 0, rows] for q in range(4)]
             mean = (means[0] + means[1] + means[2] + means[3]) * 0.25
-            square = jnp.zeros((16, 1), F32)
+            square = jnp.zeros((32, 128), F32)
             for q in range(4):
                 off = means[q] - mean
-                square += stat[q, 1, rows][:, :1] + QUART * off * off
+                square += stat[q, 1, rows] + QUART * off * off
             inv = lax.rsqrt(square / WIDTH + 1e-6)
             for q in range(4):
-                d = (cur[it, q, rows].astype(F32) - mean) * inv
-                shift = mods[q, pl.ds(step, 1)]
-                scale = mods[4 + q, pl.ds(step, 1)]
-                y[q, rows] = (d * (1.0 + scale) + shift).astype(BF16)
-            return carry
-
-        lax.fori_loop(0, 16, body, 0)
+                for c in range(5):
+                    cols = pl.ds(256 * c, 256)
+                    m2 = jnp.concatenate([mean, mean], axis=1)
+                    i2 = jnp.concatenate([inv, inv], axis=1)
+                    d = (cur[it, q, rows, cols].astype(F32) - m2) * i2
+                    shift = mods[q, pl.ds(step, 1), cols]
+                    scale = mods[4 + q, pl.ds(step, 1), cols]
+                    y[q, rows, cols] = (d * (1.0 + scale) + shift).astype(BF16)
+            return carry
+
+        lax.fori_loop(0, 8, body, 0)
 
     def project(k):
         def body(q, carry):
@@ -292,9 +301,24 @@
         lax.fori_loop(0, 4, body, 0)
         qkv[k] = acc[...].astype(BF16)
 
-    def attention(it):
+    def project_block(c):
+        cols = blocks[c]
+
+        def body(k, carry):
+            total = None
+            for q in range(4):
+                new = jnp.dot(
+                    y[q], w[k, pl.ds(q * QUART, QUART), cols], preferred_element_type=F32
+                )
+                total = new if total is None else total + new
+            qkv[k, :, cols] = total.astype(BF16)
+            return carry
+
+        lax.fori_loop(0, 3, body, 0)
+
+    def attention_block(it, c):
         for step in range(2):
-            for h in range(HEADS):
+            for n, h in enumerate(block_heads[c]):
                 rows, cols = pl.ds(TOK * step, TOK), pl.ds(HEAD_SIZE * h, HEAD_SIZE)
                 s = lax.dot_general(
                     qkv[0, rows, cols], qkv[1, rows, cols], (((1,), (1,)), ((), ())),
@@ -302,35 +326,46 @@
                 ) * (1.0 / math.sqrt(HEAD_SIZE))
                 e = jnp.exp(s - jnp.max(s, axis=-1, keepdims=True))
                 p = (e / jnp.sum(e, axis=-1, keepdims=True)).astype(BF16)
-                hd[it, x, rows, cols] = jnp.dot(
+                hd[c][it, x, rows, HEAD_SIZE * n : HEAD_SIZE * (n + 1)] = jnp.dot(
                     p, qkv[2, rows, cols], preferred_element_type=F32
                 ).astype(BF16)
-            if step == 0:
-                hd_g[it].start(0, 3)
-            else:
-                hd_g[it].start(1, 2)
+        hd_g[it][c].start(0, 3, 1, 2)
+
+    def attention(it):
+        for c in range(2):
+            attention_block(it, c)
 
     def out_part(it, q, add):
         def body(i, carry):
             rows = pl.ds(pl.multiple_of(q * QUART + i * 256, 128), 256)
             cols = pl.ds(pl.multiple_of(i * 256, 128), 256)
-            new = lax.dot_general(
-                hd[it, q], w[3, rows], (((1,), (1,)), ((), ())), preferred_element_type=F32
-            )
+            new = None
+            for c in range(2):
+                term = lax.dot_general(
+                    hd[c][it, q], w[3, rows, blocks[c]], (((1,), (1,)), ((), ())),
+                    preferred_element_type=F32,
+                )
+                new = term if new is None else new + term
             t[:, cols] = t[:, cols] + new if add else new
             return carry
 
         lax.fori_loop(0, 5, body, 0)
 
     def out_project(it):
-        g = hd_g[it]
         out_part(it, x, False)
-        g.recv(2)
+        for g in hd_g[it]:
+            g.recv(2)
         out_part(it, x3, True)
-        g.recv(3)
+        for g in hd_g[it]:
+            g.recv(3)
         out_part(it, x1, True)
-        g.recv(4, 5)
+        for g in hd_g[it]:
+            g.recv(4, 5)
         out_part(it, x2, True)
+
+    def hd_sent(it):
+        for g in hd_g[it]:
+            g.sent()
 
     first = jnp.where(tm == 0, 1.0, 0.0).astype(F32)
 
@@ -451,35 +486,42 @@
 
     def slide():
         px_msg(ITERS - 1, 8).wait_recv()
-        one = off_ref[0] == 1
         last = tm == 31
 
         def body(i, carry):
             rows = pl.ds(pl.multiple_of(16 * i, 16), 16)
             rows1 = pl.ds(pl.multiple_of(TOK + 16 * i, 16), 16)
+            rows2 = pl.ds(pl.multiple_of(2 * TOK + 16 * i, 16), 16)
             c1 = pfx[rows] + t[rows]
             c2 = c1 + t[rows1]
             c3 = c2 + sl_r[rows].astype(F32)
             c2 = jnp.where(last, c1, c2)
             c3 = jnp.where(last, c1, c3)
-            out_ref[rows] = jnp.where(one, c1, c2).astype(BF16)
-            out_ref[rows1] = jnp.where(one, c2, c3).astype(BF16)
+            out_ref[rows] = c1.astype(BF16)
+            out_ref[rows1] = c2.astype(BF16)
+            out_ref[rows2] = c3.astype(BF16)
             return carry
 
         lax.fori_loop(0, 8, body, 0)
 
+    swap_start()
     lat_g.start(0, 1, 2, 3)
     s0(0)
     s0(1)
-    s0(2)
     s1(0)
     s2(0)
+    s0(2)
+    s1(1)
+    s2(1)
+    lat_g.forward()
+    s3(0)
+    s1(2)
+    s2(2)
+    modulation()
+    s3(1)
+    s5(0)
     swap_finish()
     s0(3)
-    lat_g.forward()
-    modulation()
-    s1(1)
-    s2(1)
     block_stats(0, x)
     lat_g.recv(2, 3)
     block_stats(0, x1)
@@ -487,37 +529,33 @@
     lat_g.recv(4, 5)
     block_stats(0, x2)
     norm(0)
-
-    def weights(k, carry):
-        s3(k)
-
-        @pl.when(k < 2)
-        def _():
-            s1(k + 2)
-            s2(k + 2)
-
-        s5(k)
-        s6(k)
-        project(k)
-        return carry
-
-    lax.fori_loop(0, 3, weights, 0)
+    s6(0)
+    project(0)
+    s3(2)
+    s5(1)
+    s1(3)
+    s2(3)
+    s6(1)
+    project(1)
+    s3(3, (0,))
+    s5(2)
+    s3(3, (1, 2))
+    s6(2)
+    project(2)
     attention(0)
-    s3(3)
-    hd_g[0].forward()
+    s3(3, (3,))
+    for g in hd_g[0]:
+        g.forward()
     s5(3)
     s6(3)
     out_project(0)
     terms(0)
     t0_g.start(0, 1, 2, 3)
     prefix(0)
-    lax.fori_loop(0, 4, lambda k, c: (w_sent(k), c)[1], 0)
-    lat_g.sent()
-    hd_g[0].sent()
+    pfx_g.forward()
     t0_g.recv(2, 3, 4, 5)
     block_second(x)
     block_stats(1, x)
-    pfx_g.forward()
     pfx_g.recv(2, 3)
     for q in (x1, x3):
         block_second(q)
@@ -526,16 +564,22 @@
     block_second(x2)
     block_stats(1, x2)
     norm(1)
-    lax.fori_loop(0, 3, lambda k, c: (project(k), c)[1], 0)
-    attention(1)
-    hd_g[1].forward()
+    project_block(0)
+    attention_block(1, 0)
+    project_block(1)
+    hd_g[1][0].forward()
+    attention_block(1, 1)
+    hd_g[1][1].forward()
     out_project(1)
     terms(1)
     prefix(1)
     slide()
+    lax.fori_loop(0, 4, lambda k, c: (w_sent(k), c)[1], 0)
+    lat_g.sent()
     t0_g.sent()
     pfx_g.sent()
-    hd_g[1].sent()
+    hd_sent(0)
+    hd_sent(1)
 
 
 def features(step_index, mod_table):
@@ -556,8 +600,8 @@
     dma = pltpu.SemaphoreType.DMA
     out = pl.pallas_call(
         kernel,
-        out_shape=jax.ShapeDtypeStruct((ROWS, QUART), BF16),
-        in_specs=[hbm] * 7 + [vmem, smem, smem],
+        out_shape=jax.ShapeDtypeStruct((3 * TOK, QUART), BF16),
+        in_specs=[hbm] * 7 + [vmem, smem],
         out_specs=vmem,
         scratch_shapes=[
             pltpu.VMEM((4, WIDTH, HW), BF16),
@@ -565,7 +609,8 @@
             pltpu.VMEM((4, ROWS, QUART), BF16),
             pltpu.VMEM((ROWS, HW), F32),
             pltpu.VMEM((3, ROWS, HW), BF16),
-            pltpu.VMEM((ITERS, 4, ROWS, HW), BF16),
+            pltpu.VMEM((ITERS, 4, ROWS, 256), BF16),
+            pltpu.VMEM((ITERS, 4, ROWS, 384), BF16),
             pltpu.VMEM((4, ROWS, QUART), BF16),
             pltpu.VMEM((4, TOK, QUART), BF16),
             pltpu.VMEM((ROWS, QUART), F32),
@@ -584,13 +629,13 @@
             pltpu.VMEM((TOK, QUART), F32),
             pltpu.VMEM((TOK, QUART), BF16),
             pltpu.VMEM((TOK, QUART), BF16),
-            dma((6,)),
+            dma((7,)),
             dma((4, N_MSG)),
             dma((4, N_MSG)),
             dma((3, 6)),
             dma((3, 6)),
-            dma((ITERS, 6)),
-            dma((ITERS, 6)),
+            dma((ITERS, 2, 6)),
+            dma((ITERS, 2, 6)),
             dma((ITERS, 9)),
             dma((ITERS, 9)),
             dma,
@@ -604,9 +649,9 @@
         ),
     )(
         latents.reshape(ROWS, QUART), noise.reshape(ROWS, QUART), mod_table,
-        w_query, w_key, w_value, w_out.T, feats, hg, slide_offset.reshape(1),
+        w_query, w_key, w_value, w_out.T, feats, hg,
     )
-    return out.reshape(latents.shape)
+    return lax.dynamic_slice_in_dim(out.reshape(3, TOK, QUART), slide_offset - 1, 2, 0)
 
 
 def solution(mesh):

time: 198 us -> 187 us (0.944)
  the two profiles are of different devices: /device:TPU:1 before, /device:TPU:49 now
where the time goes in v3:
time: 187 us; the launch traced here: 186 us
  Pallas kernels  181 us (97%)
  other arithmetic  2.64 us (1%)
  local copies, waits for them, and re-layouts  1.97 us (1%)
    pallas_call x1, Pallas kernels, per_device(): pl.pallas_call(kernel, out_shape=jax.ShapeDtypeStruct((3 * TOK, QUART), B...  181 us

profile of v3, /device:TPU:49, one launch (start us, length us, event | category | flops | bytes accessed | tf_op | source)
XLA Modules:
  0.0 186.4 jit_solution(7254310848697020335)
XLA Ops:
  0.7 0.7 convert_element_type.12
  1.3 0.1 fusion.3
  1.4 0.7 add_multiply_fusion
  2.1 0.6 pad_maximum_fusion.hg_ref
  2.7 0.6 fusion.2.feats_ref
  3.3 181.1 %shard_map.91 = bf16[384,1280]{1,0:T(8,128)(2,1)} custom-call(bf16[256,1280]{1,0:T(8,128)(2,1)} %bitcast.5, bf16[256,1280]{1,0:T(8,128)(2,1)} %bitcast.6, bf16[256,15360]{1,0:T(8,128)(2,1)} %table_ref.1, bf16[160,640]{1,0:T(8,128)(2,1)} %wq_ref.1, bf16[160,640]{1,0:T(8,128)(2,1)} %wk_ref.1, bf16[160,640]{1,0:T(8,128)(2,1)} %wv_ref.1, ...), custom_call_target="tpu_custom_call" | custom-call | flops 13421772800 | bytes 12000000 | tf_op jit(solution)/shard_map/pallas_call | solution.py:601
  184.5 2.0 %constant_dynamic-slice_fusion = bf16[2,128,1280]{2,1,0:T(8,128)(2,1)} fusion(bf16[3,128,1280]{2,1,0:T(8,128)(2,1)} %bitcast.4, s32[]{:T(128)S(6)} %select_n.3), kind=kLoop, calls=%fused_computation.12 | loop fusion | bytes 1310724 | tf_op jit(solution)/shard_map/dynamic_slice | solution.py:654
  (1 shorter events, 0.0 us)

commit v4 on v3

--- a/solution.py
+++ b/solution.py
@@ -27,9 +27,9 @@
 def kernel(
     lat_ref, noise_ref, table_ref, wq_ref, wk_ref, wv_ref, wo_ref, feats_ref, hg_ref,
     out_ref,
-    w, cur, y, acc, qkv, hda, hdb, part, tb, t, nz, mods, stat,
+    w, cur, y, acc, uv, qkv, hda, hdb, part, tb, t, nz, mods, stat,
     tf, px_s, px_r, p1_s, p1_r, p2_s, p2_r, pe_s, pe_r, pfx, sl_s, sl_r,
-    loc_sem, w_ss, w_rs, ag_ss, ag_rs, hd_ss, hd_rs, px_ss, px_rs, tr_ss, tr_rs,
+    loc_sem, w_ss, w_rs, ag_ss, ag_rs, hd_ss, hd_rs, px_ss, px_rs, a_ss, a_rs, tr_ss, tr_rs,
 ):
     tm = lax.axis_index("tm")
     x = lax.axis_index("tp")
@@ -73,7 +73,7 @@
 
     barrier = pltpu.get_barrier_semaphore()
     peers = [sib, xp, xm, following, before]
-    peers += [dev(k, 0) for k in (1, 2, 3)] + [dev(0, k) for k in (1, 2, 3)]
+    peers += [(2 * lax.rem(chip + d, 16) + core, x) for d in range(1, 16)]
     for peer in peers:
         pl.semaphore_signal(barrier, inc=1, device_id=peer, device_id_type=MESH)
 
@@ -153,6 +153,7 @@
     hd = (hda, hdb)
     blocks = (pl.ds(0, 256), pl.ds(256, 384))
     block_heads = ((0, 1), (2, 3, 4))
+    whole = pl.ds(0, HW)
 
     def hd_gather(it, c):
         return Gather(
@@ -245,6 +246,10 @@
                     table_ref.at[:, pl.ds(0, QUART)], part.at[k], loc_sem.at[k]
                 ).wait()
                 mods[base + k] = jnp.dot(feats_ref[...], part[k], preferred_element_type=F32)
+        row = lax.broadcasted_iota(jnp.int32, (16, QUART), 0)
+        for q in range(4):
+            rows = jnp.where(row < 2, 1.0 + mods[4 + q], jnp.where(row < 4, mods[q], 0.0))
+            y[q, ROWS : ROWS + 16] = rows.astype(BF16)
 
     def block_stats(it, q):
         def body(i, carry):
@@ -258,14 +263,57 @@
 
         lax.fori_loop(0, 8, body, 0)
 
-    def block_second(q):
+    def prepare(q):
         def body(i, carry):
-            rows = pl.ds(pl.multiple_of(16 * i, 16), 16)
-            rows1 = pl.ds(pl.multiple_of(TOK + 16 * i, 16), 16)
-            cur[1, q, rows1] = (cur[1, q, rows].astype(F32) + tb[q, rows].astype(F32)).astype(BF16)
-            return carry
-
-        lax.fori_loop(0, 8, body, 0)
+            rows = pl.ds(pl.multiple_of(32 * i, 32), 32)
+            p = cur[1, q, rows].astype(F32)
+            for step in range(2):
+                here = pl.ds(pl.multiple_of(TOK * step + 32 * i, 32), 32)
+                c = p if step == 0 else p + tb[q, rows].astype(F32)
+                mean = jnp.sum(c, axis=-1, keepdims=True) / QUART
+                d = c - mean
+                stat[q, 0, here] = jnp.broadcast_to(mean, (32, 128))
+                stat[q, 1, here] = jnp.broadcast_to(
+                    jnp.sum(d * d, axis=-1, keepdims=True), (32, 128)
+                )
+                y[q, here] = (d * (1.0 + mods[4 + q, step : step + 1])).astype(BF16)
+            return carry
+
+        lax.fori_loop(0, 4, body, 0)
+
+    def block_project(q, cols, first=False):
+        rows = pl.ds(pl.multiple_of(q * QUART, 128), QUART)
+
+        def body(k, carry):
+            new = jnp.dot(y[q, 0:ROWS], w[k, rows, cols], preferred_element_type=F32)
+            acc[k, :, cols] = new if first else acc[k, :, cols] + new
+            return carry
+
+        lax.fori_loop(0, 3, body, 0)
+
+    def finalize(c):
+        def body(step, i, carry):
+            rows = pl.ds(pl.multiple_of(TOK * step + 32 * i, 32), 32)
+            means = [stat[q, 0, rows] for q in range(4)]
+            mean = (means[0] + means[1] + means[2] + means[3]) * 0.25
+            offs = [m - mean for m in means]
+            square = jnp.zeros((32, 128), F32)
+            for q in range(4):
+                square += stat[q, 1, rows] + QUART * offs[q] * offs[q]
+            inv = lax.rsqrt(square / WIDTH + 1e-6)
+            for k in range(3):
+                for h in block_heads[c]:
+                    cols = pl.ds(HEAD_SIZE * h, HEAD_SIZE)
+                    value = acc[k, rows, cols]
+                    add = jnp.zeros((1, HEAD_SIZE), F32)
+                    for q in range(4):
+                        value += offs[q] * uv[k, q, step : step + 1, cols]
+                        add += uv[k, q, 2 + step : 3 + step, cols]
+                    qkv[k, rows, cols] = (inv * value + add).astype(BF16)
+            return carry
+
+        for step in range(2):
+            lax.fori_loop(0, 4, functools.partial(body, step), 0)
 
     def norm(it):
         def body(i, carry):
@@ -294,27 +342,14 @@
     def project(k):
         def body(q, carry):
             rows = pl.ds(pl.multiple_of(q * QUART, 128), QUART)
-            acc[...] += jnp.dot(y[q], w[k, rows], preferred_element_type=F32)
-            return carry
-
-        acc[...] = jnp.zeros_like(acc)
+            new = jnp.dot(y[q], w[k, rows], preferred_element_type=F32)
+            acc[0] += new[:ROWS]
+            uv[k, q] = new[ROWS:]
+            return carry
+
+        acc[0] = jnp.zeros((ROWS, HW), F32)
         lax.fori_loop(0, 4, body, 0)
-        qkv[k] = acc[...].astype(BF16)
-
-    def project_block(c):
-        cols = blocks[c]
-
-        def body(k, carry):
-            total = None
-            for q in range(4):
-                new = jnp.dot(
-                    y[q], w[k, pl.ds(q * QUART, QUART), cols], preferred_element_type=F32
-                )
-                total = new if total is None else total + new
-            qkv[k, :, cols] = total.astype(BF16)
-            return carry
-
-        lax.fori_loop(0, 3, body, 0)
+        qkv[k] = acc[0].astype(BF16)
 
     def attention_block(it, c):
         for step in range(2):
@@ -398,67 +433,67 @@
     def px_msg(it, m):
         if m == 0:
             src, dst, to = px_s, px_r.at[it], sib
-        elif m < 4:
-            src, dst, to = p1_s, p1_r.at[it, m - 1], dev(m, 0)
-        elif m < 7:
-            src, dst, to = p2_s.at[m - 4], p2_r.at[it, m - 4], dev(0, m - 3)
-        elif m == 7:
+        elif m == 1:
             src, dst, to = pe_s, pe_r.at[it], sib
         else:
             src, dst, to = sl_s, sl_r, before
         return remote(src, dst, px_ss.at[it, m], px_rs.at[it, m], to)
+
+    starts = (0, 384, 768, 896)
+
+    def piece_msg(it, way, d):
+        h = lax.rem(chip + d, 16)
+        src, dst = ((p1_s, p1_r), (p2_s, p2_r))[way]
+        return remote(
+            src.at[h], dst.at[it, chip], a_ss.at[it, way, d], a_rs.at[it, way, d],
+            (2 * h + core, x),
+        )
+
+    def each(f):
+        def body(d, carry):
+            f(d)
+            return carry
+
+        lax.fori_loop(1, 16, body, 0)
 
     def prefix(it):
         px_s[...] = tf[other].astype(BF16)
         px_msg(it, 0).start()
         if it == ITERS - 1:
             sl_s[...] = t[0:TOK].astype(BF16)
-            px_msg(it, 8).start()
+            px_msg(it, 2).start()
         px_msg(it, 0).wait_recv()
 
         def loop(f):
             def body(i, carry):
-                f(pl.ds(pl.multiple_of(16 * i, 16), 16),
+                f(i, pl.ds(pl.multiple_of(16 * i, 16), 16),
                   pl.ds(pl.multiple_of(64 * core + 16 * i, 16), 16))
                 return carry
 
             lax.fori_loop(0, 4, body, 0)
 
-        def one(r, m):
-            p1_s[r] = (tf[m] + px_r[it, r].astype(F32)).astype(BF16)
+        def one(i, r, m):
+            v = (tf[m] + px_r[it, r].astype(F32)).astype(BF16)
+            for n, at in enumerate(starts):
+                p1_s[4 * i + n] = v[:, at : at + 384]
 
         loop(one)
-        for k in (1, 3, 2):
-            px_msg(it, k).start()
-        for k in (1, 3, 2):
-            px_msg(it, k).wait_recv()
+        each(lambda d: piece_msg(it, 0, d).start())
+        p1_r[it, chip] = p1_s[chip]
         if it == 0:
             t0_g.forward()
-
-        def two(r, m):
-            chip_sum = tf[m] + px_r[it, r].astype(F32)
-            lower = jnp.zeros((16, QUART), F32)
-            total = chip_sum
-            for k in (1, 2, 3):
-                there = p1_r[it, k - 1, r].astype(F32)
-                total += there
-                lower += jnp.where(k <= a, 1.0, 0.0).astype(F32) * there
-            pfx[m] = lower
-            for k in (1, 2, 3):
-                up = jnp.where(b + k < 4, 1.0, 0.0).astype(F32)
-                p2_s[k - 1, r] = (on0 * total + on1 * (lower + up * chip_sum)).astype(BF16)
-
-        loop(two)
-        for k in (4, 6, 5):
-            px_msg(it, k).start()
-        for k in (4, 6, 5):
-            px_msg(it, k).wait_recv()
-
-        def three(r, m):
-            p = pfx[m]
-            for k in (1, 2, 3):
-                keep = jnp.where(is0 & (k > b), 0.0, 1.0).astype(F32)
-                p += keep * p2_r[it, k - 1, r].astype(F32)
+        each(lambda d: piece_msg(it, 0, d).wait_recv())
+        p = jnp.zeros((16, 384), F32)
+        for g in range(16):
+            p2_s[g] = p.astype(BF16)
+            p += p1_r[it, g].astype(F32)
+        each(lambda d: piece_msg(it, 1, d).start())
+        p2_r[it, chip] = p2_s[chip]
+        each(lambda d: piece_msg(it, 1, d).wait_recv())
+
+        def three(i, r, m):
+            cut = [p2_r[it, 4 * i + n].astype(F32) for n in range(4)]
+            p = jnp.concatenate(cut[:3] + [cut[3][:, 256:]], axis=1)
             pe_s[r] = (p + on0 * tf[m]).astype(BF16)
             p += on1 * px_r[it, r].astype(F32) + first * cur[0, x, m].astype(F32)
             pfx[m] = p
@@ -466,12 +501,12 @@
                 cur[1, x, m] = p.astype(BF16)
 
         loop(three)
-        px_msg(it, 7).start()
+        px_msg(it, 1).start()
         if it == 0:
             pfx_g.start(0, 3)
-        px_msg(it, 7).wait_recv()
-
-        def four(r, m):
+        px_msg(it, 1).wait_recv()
+
+        def four(i, r, m):
             there = pl.ds(pl.multiple_of(64 - 64 * core + r.start, 16), 16)
             p = pe_r[it, r].astype(F32) + first * cur[0, x, there].astype(F32)
             pfx[there] = p
@@ -481,11 +516,13 @@
         loop(four)
         if it == 0:
             pfx_g.start(2, 1)
-        for m in range(8 + (it == ITERS - 1)):
+        for m in range(2 + (it == ITERS - 1)):
             px_msg(it, m).wait_send()
+        each(lambda d: piece_msg(it, 0, d).wait_send())
+        each(lambda d: piece_msg(it, 1, d).wait_send())
 
     def slide():
-        px_msg(ITERS - 1, 8).wait_recv()
+        px_msg(ITERS - 1, 2).wait_recv()
         last = tm == 31
 
         def body(i, carry):
@@ -552,22 +589,24 @@
     terms(0)
     t0_g.start(0, 1, 2, 3)
     prefix(0)
+    prepare(x)
     pfx_g.forward()
+    block_project(x, whole, True)
     t0_g.recv(2, 3, 4, 5)
-    block_second(x)
-    block_stats(1, x)
-    pfx_g.recv(2, 3)
-    for q in (x1, x3):
-        block_second(q)
-        block_stats(1, q)
+    pfx_g.recv(2)
+    prepare(x3)
+    block_project(x3, whole)
+    pfx_g.recv(3)
+    prepare(x1)
+    block_project(x1, whole)
     pfx_g.recv(4, 5)
-    block_second(x2)
-    block_stats(1, x2)
-    norm(1)
-    project_block(0)
+    prepare(x2)
+    block_project(x2, blocks[0])
+    finalize(0)
     attention_block(1, 0)
-    project_block(1)
+    block_project(x2, blocks[1])
     hd_g[1][0].forward()
+    finalize(1)
     attention_block(1, 1)
     hd_g[1][1].forward()
     out_project(1)
@@ -591,7 +630,7 @@
 
 def per_device(latents, noise, mod_table, w_query, w_key, w_value, w_out, step_index, slide_offset):
     feats = features(step_index, mod_table)
-    feats = jnp.concatenate([feats, jnp.zeros((14, feats.shape[1]), BF16)], axis=0)
+    feats = jnp.concatenate([feats, feats, jnp.zeros((12, feats.shape[1]), BF16)], axis=0)
     step_size = (step_index.astype(F32) + 1.0) / 2000.0
     hg = jnp.concatenate([step_size, 0.2 * jnp.sqrt(step_size)])
     hbm = pl.BlockSpec(memory_space=pl.ANY)
@@ -606,8 +645,9 @@
         scratch_shapes=[
             pltpu.VMEM((4, WIDTH, HW), BF16),
             pltpu.VMEM((ITERS, 4, ROWS, QUART), BF16),
-            pltpu.VMEM((4, ROWS, QUART), BF16),
-            pltpu.VMEM((ROWS, HW), F32),
+            pltpu.VMEM((4, ROWS + 16, QUART), BF16),
+            pltpu.VMEM((3, ROWS, HW), F32),
+            pltpu.VMEM((3, 4, 16, HW), F32),
             pltpu.VMEM((3, ROWS, HW), BF16),
             pltpu.VMEM((ITERS, 4, ROWS, 256), BF16),
             pltpu.VMEM((ITERS, 4, ROWS, 384), BF16),
@@ -620,10 +660,10 @@
             pltpu.VMEM((TOK, QUART), F32),
             pltpu.VMEM((64, QUART), BF16),
             pltpu.VMEM((ITERS, 64, QUART), BF16),
-            pltpu.VMEM((64, QUART), BF16),
-            pltpu.VMEM((ITERS, 3, 64, QUART), BF16),
-            pltpu.VMEM((3, 64, QUART), BF16),
-            pltpu.VMEM((ITERS, 3, 64, QUART), BF16),
+            pltpu.VMEM((16, 16, 384), BF16),
+            pltpu.VMEM((ITERS, 16, 16, 384), BF16),
+            pltpu.VMEM((16, 16, 384), BF16),
+            pltpu.VMEM((ITERS, 16, 16, 384), BF16),
             pltpu.VMEM((64, QUART), BF16),
             pltpu.VMEM((ITERS, 64, QUART), BF16),
             pltpu.VMEM((TOK, QUART), F32),
@@ -636,8 +676,10 @@
             dma((3, 6)),
             dma((ITERS, 2, 6)),
             dma((ITERS, 2, 6)),
-            dma((ITERS, 9)),
-            dma((ITERS, 9)),
+            dma((ITERS, 3)),
+            dma((ITERS, 3)),
+            dma((ITERS, 2, 16)),
+            dma((ITERS, 2, 16)),
             dma,
             dma,
         ],

time: 187 us -> 180 us (0.963)
  the two profiles are of different devices: /device:TPU:49 before, /device:TPU:1 now
where the time goes in v4:
time: 180 us
  Pallas kernels  174 us (97%)
  other arithmetic  2.71 us (2%)
  local copies, waits for them, and re-layouts  2.05 us (1%)
    pallas_call x1, Pallas kernels, per_device(): pl.pallas_call(kernel, out_shape=jax.ShapeDtypeStruct((3 * TOK, QUART), B...  174 us

profile of v4, /device:TPU:1, one launch (start us, length us, event | category | flops | bytes accessed | tf_op | source)
XLA Modules:
  0.0 179.5 jit_solution(7905973344740635668)
XLA Ops:
  0.7 0.7 convert_element_type.12
  1.3 0.1 pad.6.clone
  1.4 0.1 fusion
  1.5 0.7 add_multiply_fusion
  2.2 0.6 pad_maximum_fusion.hg_ref
  2.8 0.7 maximum_maximum_fusion.feats_ref
  3.5 174.1 %shard_map.91 = bf16[384,1280]{1,0:T(8,128)(2,1)} custom-call(bf16[256,1280]{1,0:T(8,128)(2,1)} %bitcast.5, bf16[256,1280]{1,0:T(8,128)(2,1)} %bitcast.6, bf16[256,15360]{1,0:T(8,128)(2,1)} %table_ref.1, bf16[160,640]{1,0:T(8,128)(2,1)} %wq_ref.1, bf16[160,640]{1,0:T(8,128)(2,1)} %wk_ref.1, bf16[160,640]{1,0:T(8,128)(2,1)} %wv_ref.1, ...), custom_call_target="tpu_custom_call" | custom-call | flops 13421772800 | bytes 12000000 | tf_op jit(solution)/shard_map/pallas_call | solution.py:640
  177.5 2.0 %constant_dynamic-slice_fusion = bf16[2,128,1280]{2,1,0:T(8,128)(2,1)} fusion(bf16[3,128,1280]{2,1,0:T(8,128)(2,1)} %bitcast.4, s32[]{:T(128)S(6)} %select_n.3), kind=kLoop, calls=%fused_computation.9 | loop fusion | bytes 1310724 | tf_op jit(solution)/shard_map/dynamic_slice | solution.py:696
  (2 shorter events, 0.0 us)

commit v5 on v4

--- a/solution.py
+++ b/solution.py
@@ -339,17 +339,17 @@
 
         lax.fori_loop(0, 8, body, 0)
 
-    def project(k):
+    def project(k, cols):
         def body(q, carry):
             rows = pl.ds(pl.multiple_of(q * QUART, 128), QUART)
-            new = jnp.dot(y[q], w[k, rows], preferred_element_type=F32)
-            acc[0] += new[:ROWS]
-            uv[k, q] = new[ROWS:]
-            return carry
-
-        acc[0] = jnp.zeros((ROWS, HW), F32)
+            new = jnp.dot(y[q], w[k, rows, cols], preferred_element_type=F32)
+            acc[0, :, cols] += new[:ROWS]
+            uv[k, q, :, cols] = new[ROWS:]
+            return carry
+
+        acc[0, :, cols] = jnp.zeros((ROWS, cols.size), F32)
         lax.fori_loop(0, 4, body, 0)
-        qkv[k] = acc[0].astype(BF16)
+        qkv[k, :, cols] = acc[0, :, cols].astype(BF16)
 
     def attention_block(it, c):
         for step in range(2):
@@ -364,11 +364,7 @@
                 hd[c][it, x, rows, HEAD_SIZE * n : HEAD_SIZE * (n + 1)] = jnp.dot(
                     p, qkv[2, rows, cols], preferred_element_type=F32
                 ).astype(BF16)
-        hd_g[it][c].start(0, 3, 1, 2)
-
-    def attention(it):
-        for c in range(2):
-            attention_block(it, c)
+        hd_g[it][c].start(0, 1, 2, 3)
 
     def out_part(it, q, add):
         def body(i, carry):
@@ -503,7 +499,7 @@
         loop(three)
         px_msg(it, 1).start()
         if it == 0:
-            pfx_g.start(0, 3)
+            pfx_g.start(0)
         px_msg(it, 1).wait_recv()
 
         def four(i, r, m):
@@ -515,7 +511,7 @@
 
         loop(four)
         if it == 0:
-            pfx_g.start(2, 1)
+            pfx_g.start(1, 2, 3)
         for m in range(2 + (it == ITERS - 1)):
             px_msg(it, m).wait_send()
         each(lambda d: piece_msg(it, 0, d).wait_send())
@@ -567,19 +563,21 @@
     block_stats(0, x2)
     norm(0)
     s6(0)
-    project(0)
+    project(0, whole)
     s3(2)
     s5(1)
     s1(3)
     s2(3)
     s6(1)
-    project(1)
+    project(1, whole)
     s3(3, (0,))
     s5(2)
     s3(3, (1, 2))
     s6(2)
-    project(2)
-    attention(0)
+    project(2, blocks[0])
+    attention_block(0, 0)
+    project(2, blocks[1])
+    attention_block(0, 1)
     s3(3, (3,))
     for g in hd_g[0]:
         g.forward()

time: 180 us -> 177 us (0.983)
  Pallas kernels: 174 us -> 171 us
    pallas_call x1, Pallas kernels: 174 us -> 171 us  [per_device(): pl.pallas_call(kernel, out_shape=jax.ShapeDtypeStruct((3 * TOK, QUART), B...]
where the time goes in v5:
time: 177 us; the launch traced here: 176 us
  Pallas kernels  171 us (97%)
  other arithmetic  2.71 us (2%)
  local copies, waits for them, and re-layouts  2.05 us (1%)
    pallas_call x1, Pallas kernels, per_device(): pl.pallas_call(kernel, out_shape=jax.ShapeDtypeStruct((3 * TOK, QUART), B...  171 us

profile of v5, /device:TPU:1, one launch (start us, length us, event | category | flops | bytes accessed | tf_op | source)
XLA Modules:
  0.0 176.4 jit_solution(90808874880356208)
XLA Ops:
  0.7 0.7 convert_element_type.12
  1.3 0.1 pad.6.clone
  1.4 0.1 fusion
  1.5 0.7 add_multiply_fusion
  2.2 0.6 pad_maximum_fusion.hg_ref
  2.8 0.7 maximum_maximum_fusion.feats_ref
  3.5 170.9 %shard_map.91 = bf16[384,1280]{1,0:T(8,128)(2,1)} custom-call(bf16[256,1280]{1,0:T(8,128)(2,1)} %bitcast.5, bf16[256,1280]{1,0:T(8,128)(2,1)} %bitcast.6, bf16[256,15360]{1,0:T(8,128)(2,1)} %table_ref.1, bf16[160,640]{1,0:T(8,128)(2,1)} %wq_ref.1, bf16[160,640]{1,0:T(8,128)(2,1)} %wk_ref.1, bf16[160,640]{1,0:T(8,128)(2,1)} %wv_ref.1, ...), custom_call_target="tpu_custom_call" | custom-call | flops 13421772800 | bytes 12000000 | tf_op jit(solution)/shard_map/pallas_call | solution.py:638
  174.4 2.0 %constant_dynamic-slice_fusion = bf16[2,128,1280]{2,1,0:T(8,128)(2,1)} fusion(bf16[3,128,1280]{2,1,0:T(8,128)(2,1)} %bitcast.4, s32[]{:T(128)S(6)} %select_n.3), kind=kLoop, calls=%fused_computation.9 | loop fusion | bytes 1310724 | tf_op jit(solution)/shard_map/dynamic_slice | solution.py:694
  (2 shorter events, 0.0 us)

commit v6 on v5

--- a/solution.py
+++ b/solution.py
@@ -25,7 +25,7 @@
 
 
 def kernel(
-    lat_ref, noise_ref, table_ref, wq_ref, wk_ref, wv_ref, wo_ref, feats_ref, hg_ref,
+    lat_ref, noise_ref, table_ref, wq_ref, wk_ref, wv_ref, wo_ref, feats_ref, index_ref,
     out_ref,
     w, cur, y, acc, uv, qkv, hda, hdb, part, tb, t, nz, mods, stat,
     tf, px_s, px_r, p1_s, p1_r, p2_s, p2_r, pe_s, pe_r, pfx, sl_s, sl_r,
@@ -404,8 +404,10 @@
         def body(i, carry):
             rows = pl.ds(pl.multiple_of(16 * i, 16), 16)
             step = lax.div(i, 8)
-            gate = mods[8, pl.ds(step, 1)] * hg_ref[step]
-            t[rows] = gate * t[rows] + hg_ref[2 + step] * nz[rows].astype(F32)
+            h = (index_ref[step].astype(F32) + 1.0) / 2000.0
+            g = 0.2 * jnp.sqrt(jnp.full((1, 1), h, F32))
+            gate = mods[8, pl.ds(step, 1)] * h
+            t[rows] = gate * t[rows] + g * nz[rows].astype(F32)
             return carry
 
         lax.fori_loop(0, 16, body, 0)
@@ -452,7 +454,7 @@
 
         lax.fori_loop(1, 16, body, 0)
 
-    def prefix(it):
+    def prefix(it, idle1, idle2):
         px_s[...] = tf[other].astype(BF16)
         px_msg(it, 0).start()
         if it == ITERS - 1:
@@ -476,8 +478,7 @@
         loop(one)
         each(lambda d: piece_msg(it, 0, d).start())
         p1_r[it, chip] = p1_s[chip]
-        if it == 0:
-            t0_g.forward()
+        idle1()
         each(lambda d: piece_msg(it, 0, d).wait_recv())
         p = jnp.zeros((16, 384), F32)
         for g in range(16):
@@ -485,6 +486,8 @@
             p += p1_r[it, g].astype(F32)
         each(lambda d: piece_msg(it, 1, d).start())
         p2_r[it, chip] = p2_s[chip]
+        idle2()
+        each(lambda d: piece_msg(it, 0, d).wait_send())
         each(lambda d: piece_msg(it, 1, d).wait_recv())
 
         def three(i, r, m):
@@ -500,6 +503,7 @@
         px_msg(it, 1).start()
         if it == 0:
             pfx_g.start(0)
+        each(lambda d: piece_msg(it, 1, d).wait_send())
         px_msg(it, 1).wait_recv()
 
         def four(i, r, m):
@@ -514,8 +518,6 @@
             pfx_g.start(1, 2, 3)
         for m in range(2 + (it == ITERS - 1)):
             px_msg(it, m).wait_send()
-        each(lambda d: piece_msg(it, 0, d).wait_send())
-        each(lambda d: piece_msg(it, 1, d).wait_send())
 
     def slide():
         px_msg(ITERS - 1, 2).wait_recv()
@@ -586,7 +588,24 @@
     out_project(0)
     terms(0)
     t0_g.start(0, 1, 2, 3)
-    prefix(0)
+
+    def idle1():
+        t0_g.forward()
+        lax.fori_loop(0, 2, lambda k, c: (w_sent(k), c)[1], 0)
+
+    def idle2():
+        lax.fori_loop(2, 4, lambda k, c: (w_sent(k), c)[1], 0)
+        lat_g.sent()
+        hd_sent(0)
+
+    def idle3():
+        t0_g.sent()
+        pfx_g.sent()
+
+    def idle4():
+        hd_sent(1)
+
+    prefix(0, idle1, idle2)
     prepare(x)
     pfx_g.forward()
     block_project(x, whole, True)
@@ -609,14 +628,8 @@
     hd_g[1][1].forward()
     out_project(1)
     terms(1)
-    prefix(1)
+    prefix(1, idle3, idle4)
     slide()
-    lax.fori_loop(0, 4, lambda k, c: (w_sent(k), c)[1], 0)
-    lat_g.sent()
-    t0_g.sent()
-    pfx_g.sent()
-    hd_sent(0)
-    hd_sent(1)
 
 
 def features(step_index, mod_table):
@@ -629,8 +642,6 @@
 def per_device(latents, noise, mod_table, w_query, w_key, w_value, w_out, step_index, slide_offset):
     feats = features(step_index, mod_table)
     feats = jnp.concatenate([feats, feats, jnp.zeros((12, feats.shape[1]), BF16)], axis=0)
-    step_size = (step_index.astype(F32) + 1.0) / 2000.0
-    hg = jnp.concatenate([step_size, 0.2 * jnp.sqrt(step_size)])
     hbm = pl.BlockSpec(memory_space=pl.ANY)
     vmem = pl.BlockSpec(memory_space=pltpu.VMEM)
     smem = pl.BlockSpec(memory_space=pltpu.SMEM)
@@ -689,7 +700,7 @@
         ),
     )(
         latents.reshape(ROWS, QUART), noise.reshape(ROWS, QUART), mod_table,
-        w_query, w_key, w_value, w_out.T, feats, hg,
+        w_query, w_key, w_value, w_out.T, feats, step_index,
     )
     return lax.dynamic_slice_in_dim(out.reshape(3, TOK, QUART), slide_offset - 1, 2, 0)
 

time: 177 us -> 175 us (0.989)
  no operation moved by 1% of the time
where the time goes in v6:
time: 175 us
  Pallas kernels  171 us (98%)
  local copies, waits for them, and re-layouts  2.05 us (1%)
    pallas_call x1, Pallas kernels, per_device(): pl.pallas_call(kernel, out_shape=jax.ShapeDtypeStruct((3 * TOK, QUART), B...  171 us

profile of v6, /device:TPU:1, one launch (start us, length us, event | category | flops | bytes accessed | tf_op | source)
XLA Modules:
  0.0 174.9 jit_solution(2933818637830791106)
XLA Ops:
  0.7 0.7 convert_element_type.11
  1.3 0.1 pad.4.clone
  1.4 0.1 fusion
  1.5 0.7 maximum_maximum_fusion.feats_ref
  2.2 170.7 %shard_map.91 = bf16[384,1280]{1,0:T(8,128)(2,1)} custom-call(bf16[256,1280]{1,0:T(8,128)(2,1)} %bitcast.5, bf16[256,1280]{1,0:T(8,128)(2,1)} %bitcast.6, bf16[256,15360]{1,0:T(8,128)(2,1)} %table_ref.1, bf16[160,640]{1,0:T(8,128)(2,1)} %wq_ref.1, bf16[160,640]{1,0:T(8,128)(2,1)} %wk_ref.1, bf16[160,640]{1,0:T(8,128)(2,1)} %wv_ref.1, ...), custom_call_target="tpu_custom_call" | custom-call | flops 13421772800 | bytes 12000000 | tf_op jit(solution)/shard_map/pallas_call | solution.py:649
  172.9 2.0 %constant_dynamic-slice_fusion = bf16[2,128,1280]{2,1,0:T(8,128)(2,1)} fusion(bf16[3,128,1280]{2,1,0:T(8,128)(2,1)} %bitcast.4, s32[]{:T(128)S(6)} %select_n.3), kind=kLoop, calls=%fused_computation.6 | loop fusion | bytes 1310724 | tf_op jit(solution)/shard_map/dynamic_slice | solution.py:705
  (2 shorter events, 0.0 us)

commit v7 on v6

--- a/solution.py
+++ b/solution.py
@@ -448,11 +448,12 @@
         )
 
     def each(f):
-        def body(d, carry):
-            f(d)
-            return carry
-
-        lax.fori_loop(1, 16, body, 0)
+        def body(i, carry):
+            for n in (1, 2, 3):
+                f(3 * i + n)
+            return carry
+
+        lax.fori_loop(0, 5, body, 0)
 
     def prefix(it, idle1, idle2):
         px_s[...] = tf[other].astype(BF16)

time: 175 us -> 175 us (level)
  no operation moved by 1% of the time
where the time goes in v7:
time: 175 us
  Pallas kernels  171 us (98%)
  local copies, waits for them, and re-layouts  2.05 us (1%)
    pallas_call x1, Pallas kernels, per_device(): pl.pallas_call(kernel, out_shape=jax.ShapeDtypeStruct((3 * TOK, QUART), B...  171 us

profile of v7, /device:TPU:1, one launch (start us, length us, event | category | flops | bytes accessed | tf_op | source)
XLA Modules:
  0.0 175.0 jit_solution(7988389752764888126)
XLA Ops:
  0.7 0.7 convert_element_type.11
  1.3 0.1 pad.4.clone
  1.4 0.1 fusion
  1.5 0.7 maximum_maximum_fusion.feats_ref
  2.2 170.9 %shard_map.91 = bf16[384,1280]{1,0:T(8,128)(2,1)} custom-call(bf16[256,1280]{1,0:T(8,128)(2,1)} %bitcast.5, bf16[256,1280]{1,0:T(8,128)(2,1)} %bitcast.6, bf16[256,15360]{1,0:T(8,128)(2,1)} %table_ref.1, bf16[160,640]{1,0:T(8,128)(2,1)} %wq_ref.1, bf16[160,640]{1,0:T(8,128)(2,1)} %wk_ref.1, bf16[160,640]{1,0:T(8,128)(2,1)} %wv_ref.1, ...), custom_call_target="tpu_custom_call" | custom-call | flops 13421772800 | bytes 12000000 | tf_op jit(solution)/shard_map/pallas_call | solution.py:650
  173.1 2.0 %constant_dynamic-slice_fusion = bf16[2,128,1280]{2,1,0:T(8,128)(2,1)} fusion(bf16[3,128,1280]{2,1,0:T(8,128)(2,1)} %bitcast.4, s32[]{:T(128)S(6)} %select_n.3), kind=kLoop, calls=%fused_computation.6 | loop fusion | bytes 1310724 | tf_op jit(solution)/shard_map/dynamic_slice | solution.py:706
  (2 shorter events, 0.0 us)
